TPU v7x, 32 devices: a whole 2x2x4 slice. The times are simulated.
32 devices in a mesh: groups: 2 (over y), region: 4 (over z), sub: 4 (over x, core).
Axes of the slice: x: 2, y: 2, z: 4, core: 2. Of those that a mesh axis runs over, the one named last changes fastest.
Arguments:
- latents: bfloat16 [32768, 128], P(('groups', 'region', 'sub')), parts along dimension 0, may hold values from -6 to 6
- cotangent: bfloat16 [32768, 128], P(('groups', 'region', 'sub')), parts along dimension 0, may hold values from -6 to 6
- inner_edges: int32 [2, 98304], P(None, ('groups', 'region', 'sub')), parts along dimension 1, may hold values from 0 to 1023
- cut_cells: int32 [24576], P(('groups', 'region', 'sub')), parts along dimension 0, may hold values from 0 to 1023
- pair_count: int32 [384], P(('groups', 'region', 'sub')), parts along dimension 0, may hold values from 0 to 64, as said below
- in_weight: bfloat16 [256, 128], replicated, may hold values from -0.375 to 0.375
- in_bias: float32 [128], replicated, may hold values from -3 to 3
- out_weight: bfloat16 [128, 128], replicated, may hold values from -0.5 to 0.5
- out_bias: float32 [128], replicated, may hold values from -3 to 3
Outputs:
- new_latents: bfloat16 [32768, 128], P(('groups', 'region', 'sub')), parts along dimension 0
- latent_grad: bfloat16 [32768, 128], P(('groups', 'region', 'sub')), parts along dimension 0
- in_weight_step: float32 [512, 128], P('groups'), parts along dimension 0
- in_bias_step: float32 [256], P('groups'), parts along dimension 0
- out_weight_step: float32 [256, 128], P('groups'), parts along dimension 0
- out_bias_step: float32 [256], P('groups'), parts along dimension 0
There are 2 independent parts, one for each index of `groups`. A program takes and returns all parts, laid end to end along the dimension named above; an argument that names none is the same for every part. Nothing has to cross between parts.
Inputs may be any that keep to these rules, and one draw needn't show every extreme that they name: `inner_edges`: local cell numbers within the subdomain that holds the edge. `cut_cells`: slot k of pair list (o, t) of subdomain p, for k below that list's count, is p's cell of the pair's k-th cut edge; the other subdomain of the pair lists the same edges in the same order. Slots at or above the count are padding. `pair_count`: the count of pair list (o, t) of subdomain p counts the cut edges between p and the subdomain at region (region of p + o - 1) modulo the number of regions and sub t; both subdomains of a pair hold the same count, and a subdomain's list with itself has count 0.
All inputs are finite; a program needn't handle non-finite values.
Results may differ from a plain program's by a relative error of at most 0.0055.
Values may be sent and summed in bfloat16 or wider, within the bound.
A program may use at most 64 MiB of HBM per device.

v0:
```python
import jax
import jax.numpy as jnp
from jax import lax
from jax.sharding import PartitionSpec as P


def from_behind(block, axis, distance):
    devices = range(lax.axis_size(axis))
    route = [((i - distance) % len(devices), i) for i in devices]
    return lax.ppermute(block, axis, route)


def flux_forward(inputs, in_weight, in_bias, out_weight, out_bias):
    before = jnp.dot(inputs, in_weight, preferred_element_type=jnp.float32) + in_bias
    hidden = jax.nn.silu(before).astype(jnp.bfloat16)
    flux_rows = (jnp.dot(hidden, out_weight, preferred_element_type=jnp.float32) + out_bias).astype(
        jnp.bfloat16
    )
    return (before, hidden, flux_rows)


def flux_backward(before, d_flux, in_weight, out_weight):
    d_hidden = jnp.dot(d_flux, out_weight.T, preferred_element_type=jnp.float32)
    logistic = jax.nn.sigmoid(before)
    d_before = (d_hidden * logistic * (1.0 + before * (1.0 - logistic))).astype(jnp.bfloat16)
    d_inputs = jnp.dot(d_before, in_weight.T, preferred_element_type=jnp.float32).astype(
        jnp.bfloat16
    )
    return (d_before, d_inputs)


def weight_terms(inputs, hidden, d_before, d_flux):
    over_rows = (((0,), (0,)), ((), ()))
    return (
        lax.dot_general(inputs, d_before, over_rows, preferred_element_type=jnp.float32),
        jnp.sum(d_before.astype(jnp.float32), axis=0),
        lax.dot_general(hidden, d_flux, over_rows, preferred_element_type=jnp.float32),
        jnp.sum(d_flux.astype(jnp.float32), axis=0),
    )


def normalized(gradient):
    return gradient / jnp.sqrt(jnp.mean(gradient * gradient) + 1e-06)


def cell_table(cells, cell_count):
    return (cells[:, None] == jnp.arange(cell_count, dtype=jnp.int32)[None, :]).astype(jnp.bfloat16)


def pick_rows(table, data):
    return jnp.dot(table, data, preferred_element_type=jnp.float32).astype(jnp.bfloat16)


def spread_rows(table, pieces):
    return lax.dot_general(
        table, pieces, (((0,), (0,)), ((), ())), preferred_element_type=jnp.float32
    )


def route(pieces):
    crossed = lax.all_to_all(pieces, "sub", split_axis=1, concat_axis=1, tiled=True)
    landed = [crossed[1], crossed[1], crossed[1]]
    for hop_by, from_slot, to_slot in ((1, 2, 0), (-1, 0, 2)):
        landed[to_slot] = from_behind(crossed[from_slot], "region", hop_by)
    return jnp.stack(landed, axis=0)


def local(
    latents, cotangent, inner_edges, cut_cells, pair_count, in_weight, in_bias, out_weight, out_bias
):
    channels = latents.shape[1]
    cell_count = latents.shape[0]
    edge_total = inner_edges.shape[1]
    block_size = 1024
    both_fields = jnp.concatenate([latents, cotangent], axis=1)

    def edge_block(running, block_rows):
        accum, grad_sums = running
        head_table = cell_table(block_rows[0], cell_count)
        tail_table = cell_table(block_rows[1], cell_count)
        head_rows = pick_rows(head_table, both_fields)
        tail_rows = pick_rows(tail_table, both_fields)
        inputs = jnp.concatenate([head_rows[:, :channels], tail_rows[:, :channels]], axis=1)
        before, hidden, flux_rows = flux_forward(inputs, in_weight, in_bias, out_weight, out_bias)
        d_flux = (
            head_rows[:, channels:].astype(jnp.float32)
            - tail_rows[:, channels:].astype(jnp.float32)
        ).astype(jnp.bfloat16)
        d_before, d_inputs = flux_backward(before, d_flux, in_weight, out_weight)
        head_pieces = jnp.concatenate([flux_rows, d_inputs[:, :channels]], axis=1)
        tail_pieces = jnp.concatenate([-flux_rows, d_inputs[:, channels:]], axis=1)
        accum = accum + spread_rows(head_table, head_pieces) + spread_rows(tail_table, tail_pieces)
        grad_sums = jax.tree.map(jnp.add, grad_sums, weight_terms(inputs, hidden, d_before, d_flux))
        return ((accum, grad_sums), None)

    blocks = jnp.transpose(inner_edges.reshape(2, edge_total // block_size, block_size), (1, 0, 2))
    zero_sums = (
        jnp.zeros(in_weight.shape, jnp.float32),
        jnp.zeros(in_bias.shape, jnp.float32),
        jnp.zeros(out_weight.shape, jnp.float32),
        jnp.zeros(out_bias.shape, jnp.float32),
    )
    initial = (jnp.zeros((cell_count, 2 * channels), jnp.float32), zero_sums)
    (accum, grad_sums), unused = lax.scan(edge_block, initial, blocks)
    regions = lax.axis_size("region")
    subparts = lax.axis_size("sub")
    region = lax.axis_index("region")
    subpart = lax.axis_index("sub")
    slot_cells = cut_cells.reshape(3, subparts, -1)
    slot_total = slot_cells.shape[2]
    offsets = jnp.arange(3, dtype=jnp.int32)
    peer_rank = ((region + offsets - 1) % regions)[:, None] * subparts + jnp.arange(
        subparts, dtype=jnp.int32
    )[None, :]
    own_rank = region * subparts + subpart
    leading = own_rank < peer_rank
    live_slots = (
        jnp.arange(slot_total, dtype=jnp.int32)[None, None, :]
        < pair_count.reshape(3, subparts)[:, :, None]
    )
    slot_table = cell_table(cut_cells, cell_count)
    own_rows = pick_rows(slot_table, both_fields).reshape(3, subparts, slot_total, 2 * channels)
    own_latents = own_rows[..., :channels]
    own_cotangent = own_rows[..., channels:]
    incoming = route(own_rows)
    peer_latents = incoming[..., :channels]
    peer_cotangent = incoming[..., channels:]
    lead_rows = leading[:, :, None, None]
    live_wide = live_slots[..., None].astype(jnp.bfloat16)
    head_latents = jnp.where(lead_rows, own_latents, peer_latents)
    tail_latents = jnp.where(lead_rows, peer_latents, own_latents)
    head_cotangent = jnp.where(lead_rows, own_cotangent, peer_cotangent)
    tail_cotangent = jnp.where(lead_rows, peer_cotangent, own_cotangent)
    inputs = jnp.concatenate([head_latents, tail_latents], axis=3).reshape(-1, 2 * channels)
    before, hidden, flux_rows = flux_forward(inputs, in_weight, in_bias, out_weight, out_bias)
    flux_live = flux_rows.reshape(3, subparts, slot_total, channels) * live_wide
    cut_shift = jnp.where(lead_rows, flux_live, -flux_live)
    d_flux = (
        (
            (head_cotangent.astype(jnp.float32) - tail_cotangent.astype(jnp.float32))
            * live_wide.astype(jnp.float32)
        )
        .astype(jnp.bfloat16)
        .reshape(-1, channels)
    )
    d_before, d_inputs = flux_backward(before, d_flux, in_weight, out_weight)
    spread = d_inputs.reshape(3, subparts, slot_total, 2 * channels)
    cut_return = jnp.where(lead_rows, spread[..., :channels], spread[..., channels:])
    cut_pieces = jnp.concatenate([cut_shift, cut_return], axis=3).reshape(-1, 2 * channels)
    accum = accum + spread_rows(slot_table, cut_pieces)
    owned_rows = (live_slots & leading[:, :, None]).reshape(-1, 1).astype(jnp.bfloat16)
    cut_terms = weight_terms(inputs, hidden, d_before * owned_rows, d_flux * owned_rows)
    grad_sums = jax.tree.map(jnp.add, grad_sums, cut_terms)
    in_weight_sum, in_bias_sum, out_weight_sum, out_bias_sum = grad_sums
    totals = lax.psum((in_weight_sum, in_bias_sum, out_weight_sum, out_bias_sum), ("region", "sub"))
    new_latents = (latents.astype(jnp.float32) + accum[:, :channels]).astype(jnp.bfloat16)
    latent_grad = (cotangent.astype(jnp.float32) + accum[:, channels:]).astype(jnp.bfloat16)
    return (
        new_latents,
        latent_grad,
        normalized(totals[0]),
        normalized(totals[1]),
        normalized(totals[2]),
        normalized(totals[3]),
    )


def solution(mesh):
    placed = (
        P(("groups", "region", "sub"), None),
        P(("groups", "region", "sub"), None),
        P(None, ("groups", "region", "sub")),
        P(("groups", "region", "sub")),
        P(("groups", "region", "sub")),
        P(),
        P(),
        P(),
        P(),
    )
    return jax.shard_map(
        local,
        mesh=mesh,
        in_specs=placed,
        out_specs=(
            P(("groups", "region", "sub"), None),
            P(("groups", "region", "sub"), None),
            P("groups", None),
            P("groups"),
            P("groups", None),
            P("groups"),
        ),
        check_vma=False,
    )
```

profile of v0, /device:TPU:0, one launch (start us, length us, event | category | flops | bytes accessed | tf_op | source)
XLA Modules:
  0.0 187.9 jit_solution(9390286437972522823)
XLA Ops:
  7.2 1.0 constant_dynamic-update-slice_fusion.1
  8.2 1.0 constant_dynamic-update-slice_fusion
  10.7 4.2 %all-to-all-start = ((bf16[3,4,64,256]{3,2,0,1:T(8,128)(2,1)}), bf16[3,4,64,256]{3,2,0,1:T(8,128)(2,1)S(1)}, u32[]{:S(2)}, u32[]{:S(2)}) async-start(bf16[3,4,64,256]{3,2,0,1:T(8,128)(2,1)} %copy.15), calls=%async_computation | async-start | bytes 786432 | tf_op jit(solution)/shard_map/all_to_all | solution.py:61
  15.1 19.9 %while.19 = (s32[]{:T(128)}, f32[1024,256]{1,0:T(8,128)S(1)}, f32[256,128]{1,0:T(8,128)S(1)}, f32[128]{0:T(128)S(1)}, f32[128,128]{1,0:T(8,128)S(1)}, /*index=5*...) while((s32[]{:T(128)}, f32[1024,256]{1,0:T(8,128)S(1)}, ...), condition=%wide.region_3.4_spmd.clone, body=%wide.region_0.3_spmd.clone.sunk | while | flops 2466087424 | bytes 16356534 | solution.py:104
  15.1 0.8 constant_dynamic-slice_fusion.3
  15.9 0.8 fusion.115
  16.7 0.8 fusion.116
  19.8 1.0 fusion.119
  20.7 1.0 fusion.120
  21.7 0.8 constant_dynamic-slice_fusion.3
  22.5 0.8 fusion.115
  23.4 0.8 fusion.116
  26.4 1.0 fusion.119
  27.4 1.0 fusion.120
  29.2 0.8 fusion.115
  30.0 0.8 fusion.116
  33.1 1.0 fusion.119
  34.1 1.0 fusion.120
  35.2 2.4 %collective-permute-start = (bf16[4,64,256]{2,1,0:T(8,128)(2,1)S(1)}, bf16[4,64,256]{2,1,0:T(8,128)(2,1)S(1)}, u32[]{:S(2)}, u32[]{:S(2)}) collective-permute-start(bf16[4,64,256]{2,1,0:T(8,128)(2,1)S(1)} %get-tuple-element.162), channel_id=1, source_target_pairs={{12,0},{0,4},{4,8},{8,12},{13,1},{1,5},{5,9},{9,13},{14,2},{2,6},{... | collective-permute-start | bytes 393224 | tf_op jit(solution)/shard_map/ppermute | solution.py:10
  37.6 2.1 %collective-permute-start.1 = (bf16[4,64,256]{2,1,0:T(8,128)(2,1)S(1)}, bf16[4,64,256]{2,1,0:T(8,128)(2,1)S(1)}, u32[]{:S(2)}, u32[]{:S(2)}) collective-permute-start(bf16[4,64,256]{2,1,0:T(8,128)(2,1)S(1)} %get-tuple-element.163), channel_id=1, source_target_pairs={{4,0},{8,4},{12,8},{0,12},{5,1},{9,5},{13,9},{1,13},{6,2},{10,6},{... | collective-permute-start | bytes 393224 | tf_op jit(solution)/shard_map/ppermute | solution.py:10
  39.9 4.1 %collective-permute-done = bf16[4,64,256]{2,1,0:T(8,128)(2,1)S(1)} collective-permute-done((bf16[4,64,256]{2,1,0:T(8,128)(2,1)S(1)}, bf16[4,64,256]{2,1,0:T(8,128)(2,1)S(1)}, u32[]{:S(2)}, u32[]{:S(2)}) %collective-permute-start) | collective-permute-done | bytes 131104 | tf_op jit(solution)/shard_map/ppermute | solution.py:10
  44.0 1.9 %collective-permute-done.1 = bf16[4,64,256]{2,1,0:T(8,128)(2,1)S(1)} collective-permute-done((bf16[4,64,256]{2,1,0:T(8,128)(2,1)S(1)}, bf16[4,64,256]{2,1,0:T(8,128)(2,1)S(1)}, u32[]{:S(2)}, u32[]{:S(2)}) %collective-permute-start.1) | collective-permute-done | bytes 131104 | tf_op jit(solution)/shard_map/ppermute | solution.py:10
  47.6 1.0 convolution_add_fusion.7
  48.6 1.1 convolution_add_fusion.6
  49.7 31.7 %all-reduce = (f32[128]{0:T(128)S(1)}, f32[128]{0:T(128)S(1)}) all-reduce(f32[128]{0:T(128)S(1)} %add.177, f32[128]{0:T(128)S(1)} %add.181), channel_id=1, replica_groups=mesh['groups'=2,'region'=4,'sub'=4] {'region','sub'}, use_global_device_ids=true, to_apply=%region_7.8 | all-reduce | flops 256 | bytes 2048 | tf_op jit(solution)/shard_map/psum | solution.py:155
  84.2 1.1 fusion.39
  85.3 0.9 fusion.44
  86.8 86.8 %all-reduce.4.cloned.1.call-done = (f32[256,128]{1,0:T(8,128)}, f32[128,128]{1,0:T(8,128)}) async-done(((f32[256,128]{1,0:T(8,128)}, f32[128,128]{1,0:T(8,128)}), (f32[256,128]{1,0:T(8,128)}, f32[128,128]{1,0:T(8,128)})) %all-reduce.4.cloned.1.call-update) | async-done | bytes 196624 | tf_op jit(solution)/shard_map/psum | solution.py:155
  173.6 1.5 multiply_reduce_fusion.1
  175.7 1.5 multiply_reduce_fusion
  178.0 1.6 broadcast_divide_fusion
  179.6 1.5 broadcast_divide_fusion.1
  (81 shorter events, 12.6 us)
Async XLA Ops:
  7.2 2.0 %copy-start.6 = (s32[768]{0:T(1024)S(1)}, s32[768]{0:T(1024)}, u32[]{:S(2)}) copy-start(s32[768]{0:T(1024)} %param.14) | copy-start | bytes 9220
  9.9 5.1 %copy-start.5 = (s32[12]{0:T(128)S(1)}, s32[12]{0:T(128)}, u32[]{:S(2)}) copy-start(s32[12]{0:T(128)} %param.15) | copy-start | bytes 148
  9.9 5.2 %copy-start = (bf16[256,128]{1,0:T(8,128)(2,1)S(1)}, bf16[256,128]{1,0:T(8,128)(2,1)}, u32[]{:S(2)}) copy-start(bf16[256,128]{1,0:T(8,128)(2,1)} %param.16) | copy-start | bytes 196612
  9.9 5.1 %copy-start.1 = (bf16[128,128]{1,0:T(8,128)(2,1)S(1)}, bf16[128,128]{1,0:T(8,128)(2,1)}, u32[]{:S(2)}) copy-start(bf16[128,128]{1,0:T(8,128)(2,1)} %param.18) | copy-start | bytes 98308
  9.9 5.1 %copy-start.4 = (f32[128]{0:T(128)S(1)}, f32[128]{0:T(128)}, u32[]{:S(2)}) copy-start(f32[128]{0:T(128)} %param.19) | copy-start | bytes 1540
  9.9 5.1 %copy-start.7 = (f32[128]{0:T(128)S(1)}, f32[128]{0:T(128)}, u32[]{:S(2)}) copy-start(f32[128]{0:T(128)} %param.17) | copy-start | bytes 1540
  10.7 24.4 %all-to-all-start = ((bf16[3,4,64,256]{3,2,0,1:T(8,128)(2,1)}), bf16[3,4,64,256]{3,2,0,1:T(8,128)(2,1)S(1)}, u32[]{:S(2)}, u32[]{:S(2)}) async-start(bf16[3,4,64,256]{3,2,0,1:T(8,128)(2,1)} %copy.15), calls=%async_computation | async-start | bytes 786432 | tf_op jit(solution)/shard_map/all_to_all | solution.py:61
  14.9 158.7 %all-reduce.4.cloned.1.call-start = ((), (), s32[]{:S(2)}) async-start(), calls=%async_computation.1 | async-start | bytes 393216 | tf_op jit(solution)/shard_map/psum | solution.py:155
  35.2 8.8 %collective-permute-start = (bf16[4,64,256]{2,1,0:T(8,128)(2,1)S(1)}, bf16[4,64,256]{2,1,0:T(8,128)(2,1)S(1)}, u32[]{:S(2)}, u32[]{:S(2)}) collective-permute-start(bf16[4,64,256]{2,1,0:T(8,128)(2,1)S(1)} %get-tuple-element.162), channel_id=1, source_target_pairs={{12,0},{0,4},{4,8},{8,12},{13,1},{1,5},{5,9},{9,13},{14,2},{2,6},{... | collective-permute-start | bytes 393224 | tf_op jit(solution)/shard_map/ppermute | solution.py:10
  37.6 8.4 %collective-permute-start.1 = (bf16[4,64,256]{2,1,0:T(8,128)(2,1)S(1)}, bf16[4,64,256]{2,1,0:T(8,128)(2,1)S(1)}, u32[]{:S(2)}, u32[]{:S(2)}) collective-permute-start(bf16[4,64,256]{2,1,0:T(8,128)(2,1)S(1)} %get-tuple-element.163), channel_id=1, source_target_pairs={{4,0},{8,4},{12,8},{0,12},{5,1},{9,5},{13,9},{1,13},{6,2},{10,6},{... | collective-permute-start | bytes 393224 | tf_op jit(solution)/shard_map/ppermute | solution.py:10
  84.2 1.2 copy-start.2
  84.2 1.2 copy-start.3
Sparse Core Ops, SparseCore 0:
  86.4 87.1 all-reduce.3
where the time goes:
time: 189 us; the launch traced here: 188 us
  waiting for transfers between devices  92.9 us (49%)
  blocking collectives  31.7 us (17%)
  matrix products  21.5 us (11%)
  between operations  17 us (9%)
  other arithmetic  10.1 us (5%)
  starting transfers between devices  8.73 us (5%)
  local copies, waits for them, and re-layouts  5.61 us (3%)
    psum x1, waiting for transfers between devices, local(): lax.psum((in_weight_sum, in_bias_sum, out_weight_sum, out_bias_sum), ('re...  86.8 us
    psum x1, blocking collectives, local(): lax.psum((in_weight_sum, in_bias_sum, out_weight_sum, out_bias_sum), ('re...  31.7 us
    dot_general x7, matrix products, spread_rows(): lax.dot_general(table, pieces, (((0,), (0,)), ((), ())), preferred_elemen...  6.95 us
    ppermute x2, waiting for transfers between devices, from_behind(): return lax.ppermute(block, axis, route)  6.06 us
    dot_general x7, matrix products, pick_rows(): jnp.dot(table, data, preferred_element_type=jnp.float32)  5.7 us
    ppermute x2, starting transfers between devices, from_behind(): return lax.ppermute(block, axis, route)  4.52 us
    all_to_all x1, starting transfers between devices, route(): lax.all_to_all(pieces, 'sub', split_axis=1, concat_axis=1, tiled=True)  4.21 us
    div x4, other arithmetic, normalized(): return gradient / jnp.sqrt(jnp.mean(gradient * gradient) + 1e-06)  4.09 us
  transfers between devices with their start and end apart: 4, of which 3 were waited for; matrix products, arithmetic and copies ran while one was open for 11% of the time, Pallas kernels for 0%

commit v1 on v0

--- a/solution.py
+++ b/solution.py
@@ -1,7 +1,145 @@
+import functools
+
 import jax
 import jax.numpy as jnp
 from jax import lax
+from jax.experimental import pallas as pl
+from jax.experimental.pallas import tpu as pltpu
 from jax.sharding import PartitionSpec as P
+
+MESH = pl.DeviceIdType.MESH
+
+
+def round_up(value, step):
+    return -(-value // step) * step
+
+
+def device_at(rank, subparts):
+    return {"region": rank // subparts, "sub": lax.rem(rank, subparts)}
+
+
+def high_low(value):
+    high = value.astype(jnp.bfloat16).astype(jnp.float32)
+    return high, value - high
+
+
+def greet_all(me, total, subparts):
+    barrier = pltpu.get_barrier_semaphore()
+
+    def greet(step, unused):
+        peer = lax.rem(me + step, total)
+        pl.semaphore_signal(barrier, inc=1, device_id=device_at(peer, subparts), device_id_type=MESH)
+        return unused
+
+    lax.fori_loop(1, total, greet, 0)
+    pl.semaphore_wait(barrier, total - 1)
+
+
+def exchange(me, total, subparts, source, target, send_sem, recv_sem):
+    def copy_of(step):
+        peer = lax.rem(me + step, total)
+        return pltpu.make_async_remote_copy(
+            src_ref=source(peer),
+            dst_ref=target(step),
+            send_sem=send_sem.at[step],
+            recv_sem=recv_sem.at[step],
+            device_id=device_at(peer, subparts),
+            device_id_type=MESH,
+        )
+
+    def begin(step, unused):
+        copy_of(step).start()
+        return unused
+
+    def finish(step, unused):
+        copy_of(step).wait()
+        return unused
+
+    return (
+        lambda: lax.fori_loop(1, total, begin, 0),
+        lambda: lax.fori_loop(1, total, finish, 0),
+    )
+
+
+def sum_kernel(
+    regions, subparts, chunk,
+    in_weight, in_bias, out_weight, out_bias,
+    in_weight_out, in_bias_out, out_weight_out, out_bias_out,
+    terms, sent, landed, gathered, send_a, recv_a, send_b, recv_b,
+):
+    total = regions * subparts
+    me = lax.axis_index("region") * subparts + lax.axis_index("sub")
+    slot_rows = sent.shape[1]
+    wide = in_weight.shape[0]
+    narrow = out_weight.shape[0]
+    greet_all(me, total, subparts)
+    terms[0:wide] = in_weight[...]
+    terms[wide : wide + narrow] = out_weight[...]
+    terms[wide + narrow :] = jnp.zeros((terms.shape[0] - wide - narrow, terms.shape[1]), jnp.float32)
+    bias_rows = jnp.concatenate(
+        [*high_low(in_bias[...]), *high_low(out_bias[...]),
+         jnp.zeros((slot_rows - chunk - 4, terms.shape[1]), jnp.float32)], axis=0
+    )
+
+    def fill(rank, unused):
+        part = terms[pl.ds(pl.multiple_of(rank * chunk, 8), chunk)]
+        sent[rank] = jnp.concatenate([part, bias_rows], axis=0).astype(jnp.bfloat16)
+        return unused
+
+    lax.fori_loop(0, total, fill, 0)
+    begin, finish = exchange(
+        me, total, subparts, lambda peer: sent.at[peer], lambda step: landed.at[step], send_a, recv_a
+    )
+    begin()
+    landed[0] = sent[me]
+    finish()
+    owned = jnp.sum(landed[...].astype(jnp.float32), axis=0)
+    gathered[me] = owned.astype(jnp.bfloat16)
+    begin, finish = exchange(
+        me, total, subparts, lambda peer: gathered.at[me], lambda step: gathered.at[me], send_b, recv_b
+    )
+    begin()
+    in_bias_out[...] = normalized(owned[chunk : chunk + 1] + owned[chunk + 1 : chunk + 2])
+    out_bias_out[...] = normalized(owned[chunk + 2 : chunk + 3] + owned[chunk + 3 : chunk + 4])
+    finish()
+    everything = gathered[...].astype(jnp.float32)[:, :chunk].reshape(total * chunk, -1)
+    in_weight_out[...] = normalized(everything[:wide])
+    out_weight_out[...] = normalized(everything[wide : wide + narrow])
+
+
+def summed_steps(in_weight, in_bias, out_weight, out_bias):
+    regions = lax.axis_size("region")
+    subparts = lax.axis_size("sub")
+    total = regions * subparts
+    wide, lanes = in_weight.shape
+    narrow = out_weight.shape[0]
+    chunk = round_up(-(-(wide + narrow) // total), 8)
+    slot_rows = round_up(chunk + 4, 16)
+    vmem = pl.BlockSpec(memory_space=pltpu.VMEM)
+    f32 = jnp.float32
+    a, b, c, d = pl.pallas_call(
+        functools.partial(sum_kernel, regions, subparts, chunk),
+        out_shape=[
+            jax.ShapeDtypeStruct((wide, lanes), f32),
+            jax.ShapeDtypeStruct((1, lanes), f32),
+            jax.ShapeDtypeStruct((narrow, out_weight.shape[1]), f32),
+            jax.ShapeDtypeStruct((1, out_weight.shape[1]), f32),
+        ],
+        in_specs=[vmem] * 4,
+        out_specs=[vmem] * 4,
+        scratch_shapes=[
+            pltpu.VMEM((max(total * chunk, wide + narrow + 8), lanes), f32),
+            pltpu.VMEM((total, slot_rows, lanes), jnp.bfloat16),
+            pltpu.VMEM((total, slot_rows, lanes), jnp.bfloat16),
+            pltpu.VMEM((total, slot_rows, lanes), jnp.bfloat16),
+            pltpu.SemaphoreType.DMA((total,)),
+            pltpu.SemaphoreType.DMA((total,)),
+            pltpu.SemaphoreType.DMA((total,)),
+            pltpu.SemaphoreType.DMA((total,)),
+        ],
+        compiler_params=pltpu.CompilerParams(collective_id=0, has_side_effects=True),
+    )(in_weight, in_bias[None], out_weight, out_bias[None])
+    return a, b[0], c, d[0]
 
 
 def from_behind(block, axis, distance):
@@ -152,16 +290,13 @@
     cut_terms = weight_terms(inputs, hidden, d_before * owned_rows, d_flux * owned_rows)
     grad_sums = jax.tree.map(jnp.add, grad_sums, cut_terms)
     in_weight_sum, in_bias_sum, out_weight_sum, out_bias_sum = grad_sums
-    totals = lax.psum((in_weight_sum, in_bias_sum, out_weight_sum, out_bias_sum), ("region", "sub"))
+    steps = summed_steps(in_weight_sum, in_bias_sum, out_weight_sum, out_bias_sum)
     new_latents = (latents.astype(jnp.float32) + accum[:, :channels]).astype(jnp.bfloat16)
     latent_grad = (cotangent.astype(jnp.float32) + accum[:, channels:]).astype(jnp.bfloat16)
     return (
         new_latents,
         latent_grad,
-        normalized(totals[0]),
-        normalized(totals[1]),
-        normalized(totals[2]),
-        normalized(totals[3]),
+        *steps,
     )
 
 

time: 189 us -> 64.4 us (0.34)
  waiting for transfers between devices: 92.9 us -> 6.08 us
  blocking collectives: 31.7 us -> 0 us
  between operations: 17 us -> 0.89 us
  Pallas kernels: 0 us -> 15.6 us
  other arithmetic: 10.1 us -> 2.92 us
  local copies, waits for them, and re-layouts: 5.61 us -> 7.94 us
    psum x1 -> x0, waiting for transfers between devices: 86.8 us -> none  [local(): lax.psum((in_weight_sum, in_bias_sum, out_weight_sum, out_bias_sum), ('re...]
    psum x1 -> x0, blocking collectives: 31.7 us -> none  [local(): lax.psum((in_weight_sum, in_bias_sum, out_weight_sum, out_bias_sum), ('re...]
    pallas_call x0 -> x1, Pallas kernels: none -> 15.6 us  [summed_steps(): pl.pallas_call(functools.partial(sum_kernel, regions, subparts, chunk), o...]
    div x4 -> x0, other arithmetic: 4.09 us -> none  [normalized(): return gradient / jnp.sqrt(jnp.mean(gradient * gradient) + 1e-06)]
    reduce_sum x3 -> x0, other arithmetic: 3.61 us -> none  [normalized(): return gradient / jnp.sqrt(jnp.mean(gradient * gradient) + 1e-06)]
    unnamed x17 -> x29, local copies, waits for them, and re-layouts: 1.05 us -> 3.37 us
  transfers between devices with their start and end apart: 4 -> 3, of which waited for: 3 -> 2; matrix products, arithmetic and copies ran while one was open for 11% -> 31% of each run, Pallas kernels for 0% -> 0%
where the time goes in v1:
time: 64.4 us; the launch traced here: 63.9 us
  matrix products  21.4 us (33%)
  Pallas kernels  15.6 us (24%)
  starting transfers between devices  8.7 us (14%)
  local copies, waits for them, and re-layouts  7.94 us (12%)
  waiting for transfers between devices  6.08 us (9%)
  other arithmetic  2.92 us (5%)
  between operations  0.89 us (1%)
    pallas_call x1, Pallas kernels, summed_steps(): pl.pallas_call(functools.partial(sum_kernel, regions, subparts, chunk), o...  15.6 us
    dot_general x7, matrix products, spread_rows(): lax.dot_general(table, pieces, (((0,), (0,)), ((), ())), preferred_elemen...  6.94 us
    ppermute x2, waiting for transfers between devices, from_behind(): return lax.ppermute(block, axis, route)  6.08 us
    dot_general x7, matrix products, pick_rows(): jnp.dot(table, data, preferred_element_type=jnp.float32)  5.69 us
    ppermute x2, starting transfers between devices, from_behind(): return lax.ppermute(block, axis, route)  4.49 us
    all_to_all x1, starting transfers between devices, route(): lax.all_to_all(pieces, 'sub', split_axis=1, concat_axis=1, tiled=True)  4.21 us
    unnamed x29, local copies, waits for them, and re-layouts  3.37 us
    slice x3, local copies, waits for them, and re-layouts, edge_block(): tail_table = cell_table(block_rows[1], cell_count)  2.36 us
  transfers between devices with their start and end apart: 3, of which 2 were waited for; matrix products, arithmetic and copies ran while one was open for 31% of the time, Pallas kernels for 0%

profile of v1, /device:TPU:0, one launch (start us, length us, event | category | flops | bytes accessed | tf_op | source)
XLA Modules:
  0.0 63.9 jit_solution(12714123093398113255)
XLA Ops:
  0.6 1.0 %constant_dynamic-update-slice_fusion.1 = bf16[1024,256]{1,0:T(8,128)(2,1)S(1)} fusion(bf16[1024,128]{1,0:T(8,128)(2,1)} %param.11), kind=kLoop, calls=%fused_computation.87 | loop fusion | bytes 524288
  1.6 1.0 %constant_dynamic-update-slice_fusion = bf16[1024,256]{1,0:T(8,128)(2,1)S(1)} fusion(bf16[1024,256]{1,0:T(8,128)(2,1)S(1)} %constant_dynamic-update-slice_fusion.1, bf16[1024,128]{1,0:T(8,128)(2,1)} %param.12), kind=kLoop, calls=%fused_computation.86 | loop fusion | bytes 524288 | tf_op jit(solution)/shard_map/concatenate | solution.py:213
  2.7 0.7 %fusion.40 = bf16[768,256]{1,0:T(8,128)(2,1)S(1)} fusion(bf16[1024,256]{1,0:T(8,128)(2,1)S(1)} %constant_dynamic-update-slice_fusion, s32[768]{0:T(1024)S(1)} %copy-done.8), kind=kOutput, calls=%fused_computation.53 | convolution fusion | flops 403636224 | bytes 920576 | tf_op jit(solution)/shard_map/dot_general | solution.py:189
  3.4 0.8 %copy.15 = bf16[3,4,64,256]{3,2,0,1:T(8,128)(2,1)} copy(bf16[3,4,64,256]{3,2,1,0:T(8,128)(2,1)S(1)} %bitcast.74) | data formatting | bytes 786432 | tf_op jit(solution)/shard_map/reshape | solution.py:260
  4.2 4.2 %all-to-all-start = ((bf16[3,4,64,256]{3,2,0,1:T(8,128)(2,1)}), bf16[3,4,64,256]{3,2,0,1:T(8,128)(2,1)S(1)}, u32[]{:S(2)}, u32[]{:S(2)}) async-start(bf16[3,4,64,256]{3,2,0,1:T(8,128)(2,1)} %copy.15), calls=%async_computation | async-start | bytes 786432 | tf_op jit(solution)/shard_map/all_to_all | solution.py:199
  8.5 19.9 %while.19 = (s32[]{:T(128)}, f32[1024,256]{1,0:T(8,128)S(1)}, f32[256,128]{1,0:T(8,128)S(1)}, f32[128]{0:T(128)S(1)}, f32[128,128]{1,0:T(8,128)S(1)}, /*index=5*...) while((s32[]{:T(128)}, f32[1024,256]{1,0:T(8,128)S(1)}, ...), condition=%wide.region_3.4_spmd.clone, body=%wide.region_0.3_spmd.clone.sunk | while | flops 2466087424 | bytes 16356534 | solution.py:242
  8.5 0.8 %constant_dynamic-slice_fusion.3 = (s32[1,1,1024]{2,1,0:T(1,128)S(1)}, s32[1,1,1024]{2,1,0:T(1,128)S(1)}) fusion(s32[3,2,1024]{2,1,0:T(2,128)} %get-tuple-element.313, s32[]{:T(128)S(6)} %copy.27, s32[]{:T(128)S(6)} %add.237), kind=kLoop, calls=%fused_computation.42.clone.1 | loop fusion | bytes 16392 | tf_op jit(solution)/shard_map/while/body/eval_jaxpr/slice | solution.py:218
  9.3 0.8 %fusion.115 = bf16[1024,256]{1,0:T(8,128)(2,1)S(1)} fusion(bf16[1024,256]{1,0:T(8,128)(2,1)S(1)} %get-tuple-element.314, s32[1024]{0:T(1024)S(1)} %bitcast.85), kind=kOutput, calls=%fused_computation.15.clone.1 | convolution fusion | flops 538181632 | bytes 1052672 | tf_op jit(solution)/shard_map/while/body/eval_jaxpr/dot_general | solution.py:189
  10.2 0.8 %fusion.116 = bf16[1024,256]{1,0:T(8,128)(2,1)S(1)} fusion(bf16[1024,256]{1,0:T(8,128)(2,1)S(1)} %get-tuple-element.314, s32[1024]{0:T(1024)S(1)} %bitcast.87), kind=kOutput, calls=%fused_computation.14.clone.1 | convolution fusion | flops 538181632 | bytes 1052672 | tf_op jit(solution)/shard_map/while/body/eval_jaxpr/dot_general | solution.py:189
  13.2 1.0 %fusion.119 = f32[1024,256]{1,0:T(8,128)S(1)} fusion(s32[1024]{0:T(1024)S(1)} %bitcast.88, f32[1024,256]{1,0:T(8,128)S(1)} %get-tuple-element.293, bf16[1024,128]{0,1:T(8,128)(2,1)S(1)} %get-tuple-element.269, bf16[1024,128]{0,1:T(8,128)(2,1)S(1)} %get-tuple-element.271, pred[]{:T(512)S(6)} %compare.7), kind=kOutput, calls=%fused_computation.13.clone.1 | convolution fusion | flops 540540928 | bytes 2625537 | tf_op jit(solution)/shard_map/while/body/eval_jaxpr/dot_general | solution.py:193
  14.2 1.0 %fusion.120 = f32[1024,256]{1,0:T(8,128)S(1)} fusion(f32[1024,256]{1,0:T(8,128)S(1)} %fusion.119, s32[1024]{0:T(1024)S(1)} %bitcast.86, bf16[1024,128]{0,1:T(8,128)(2,1)S(1)} %get-tuple-element.272, bf16[1024,128]{0,1:T(8,128)(2,1)S(1)} %get-tuple-element.273), kind=kOutput, calls=%fused_computation.12.clone.1 | convolution fusion | flops 540278784 | bytes 2625536 | tf_op jit(solution)/shard_map/while/body/eval_jaxpr/dot_general | solution.py:193
  15.2 0.8 %constant_dynamic-slice_fusion.3 = (s32[1,1,1024]{2,1,0:T(1,128)S(1)}, s32[1,1,1024]{2,1,0:T(1,128)S(1)}) fusion(s32[3,2,1024]{2,1,0:T(2,128)} %get-tuple-element.313, s32[]{:T(128)S(6)} %copy.27, s32[]{:T(128)S(6)} %add.237), kind=kLoop, calls=%fused_computation.42.clone.1 | loop fusion | bytes 16392 | tf_op jit(solution)/shard_map/while/body/eval_jaxpr/slice | solution.py:218
  16.0 0.8 %fusion.115 = bf16[1024,256]{1,0:T(8,128)(2,1)S(1)} fusion(bf16[1024,256]{1,0:T(8,128)(2,1)S(1)} %get-tuple-element.314, s32[1024]{0:T(1024)S(1)} %bitcast.85), kind=kOutput, calls=%fused_computation.15.clone.1 | convolution fusion | flops 538181632 | bytes 1052672 | tf_op jit(solution)/shard_map/while/body/eval_jaxpr/dot_general | solution.py:189
  16.8 0.8 %fusion.116 = bf16[1024,256]{1,0:T(8,128)(2,1)S(1)} fusion(bf16[1024,256]{1,0:T(8,128)(2,1)S(1)} %get-tuple-element.314, s32[1024]{0:T(1024)S(1)} %bitcast.87), kind=kOutput, calls=%fused_computation.14.clone.1 | convolution fusion | flops 538181632 | bytes 1052672 | tf_op jit(solution)/shard_map/while/body/eval_jaxpr/dot_general | solution.py:189
  19.8 1.0 %fusion.119 = f32[1024,256]{1,0:T(8,128)S(1)} fusion(s32[1024]{0:T(1024)S(1)} %bitcast.88, f32[1024,256]{1,0:T(8,128)S(1)} %get-tuple-element.293, bf16[1024,128]{0,1:T(8,128)(2,1)S(1)} %get-tuple-element.269, bf16[1024,128]{0,1:T(8,128)(2,1)S(1)} %get-tuple-element.271, pred[]{:T(512)S(6)} %compare.7), kind=kOutput, calls=%fused_computation.13.clone.1 | convolution fusion | flops 540540928 | bytes 2625537 | tf_op jit(solution)/shard_map/while/body/eval_jaxpr/dot_general | solution.py:193
  20.8 1.0 %fusion.120 = f32[1024,256]{1,0:T(8,128)S(1)} fusion(f32[1024,256]{1,0:T(8,128)S(1)} %fusion.119, s32[1024]{0:T(1024)S(1)} %bitcast.86, bf16[1024,128]{0,1:T(8,128)(2,1)S(1)} %get-tuple-element.272, bf16[1024,128]{0,1:T(8,128)(2,1)S(1)} %get-tuple-element.273), kind=kOutput, calls=%fused_computation.12.clone.1 | convolution fusion | flops 540278784 | bytes 2625536 | tf_op jit(solution)/shard_map/while/body/eval_jaxpr/dot_general | solution.py:193
  21.8 0.8 %constant_dynamic-slice_fusion.3 = (s32[1,1,1024]{2,1,0:T(1,128)S(1)}, s32[1,1,1024]{2,1,0:T(1,128)S(1)}) fusion(s32[3,2,1024]{2,1,0:T(2,128)} %get-tuple-element.313, s32[]{:T(128)S(6)} %copy.27, s32[]{:T(128)S(6)} %add.237), kind=kLoop, calls=%fused_computation.42.clone.1 | loop fusion | bytes 16392 | tf_op jit(solution)/shard_map/while/body/eval_jaxpr/slice | solution.py:218
  22.6 0.8 %fusion.115 = bf16[1024,256]{1,0:T(8,128)(2,1)S(1)} fusion(bf16[1024,256]{1,0:T(8,128)(2,1)S(1)} %get-tuple-element.314, s32[1024]{0:T(1024)S(1)} %bitcast.85), kind=kOutput, calls=%fused_computation.15.clone.1 | convolution fusion | flops 538181632 | bytes 1052672 | tf_op jit(solution)/shard_map/while/body/eval_jaxpr/dot_general | solution.py:189
  23.5 0.8 %fusion.116 = bf16[1024,256]{1,0:T(8,128)(2,1)S(1)} fusion(bf16[1024,256]{1,0:T(8,128)(2,1)S(1)} %get-tuple-element.314, s32[1024]{0:T(1024)S(1)} %bitcast.87), kind=kOutput, calls=%fused_computation.14.clone.1 | convolution fusion | flops 538181632 | bytes 1052672 | tf_op jit(solution)/shard_map/while/body/eval_jaxpr/dot_general | solution.py:189
  26.5 1.0 %fusion.119 = f32[1024,256]{1,0:T(8,128)S(1)} fusion(s32[1024]{0:T(1024)S(1)} %bitcast.88, f32[1024,256]{1,0:T(8,128)S(1)} %get-tuple-element.293, bf16[1024,128]{0,1:T(8,128)(2,1)S(1)} %get-tuple-element.269, bf16[1024,128]{0,1:T(8,128)(2,1)S(1)} %get-tuple-element.271, pred[]{:T(512)S(6)} %compare.7), kind=kOutput, calls=%fused_computation.13.clone.1 | convolution fusion | flops 540540928 | bytes 2625537 | tf_op jit(solution)/shard_map/while/body/eval_jaxpr/dot_general | solution.py:193
  27.5 1.0 %fusion.120 = f32[1024,256]{1,0:T(8,128)S(1)} fusion(f32[1024,256]{1,0:T(8,128)S(1)} %fusion.119, s32[1024]{0:T(1024)S(1)} %bitcast.86, bf16[1024,128]{0,1:T(8,128)(2,1)S(1)} %get-tuple-element.272, bf16[1024,128]{0,1:T(8,128)(2,1)S(1)} %get-tuple-element.273), kind=kOutput, calls=%fused_computation.12.clone.1 | convolution fusion | flops 540278784 | bytes 2625536 | tf_op jit(solution)/shard_map/while/body/eval_jaxpr/dot_general | solution.py:193
  28.6 2.4 %collective-permute-start = (bf16[4,64,256]{2,1,0:T(8,128)(2,1)S(1)}, bf16[4,64,256]{2,1,0:T(8,128)(2,1)S(1)}, u32[]{:S(2)}, u32[]{:S(2)}) collective-permute-start(bf16[4,64,256]{2,1,0:T(8,128)(2,1)S(1)} %get-tuple-element.166), channel_id=1, source_target_pairs={{12,0},{0,4},{4,8},{8,12},{13,1},{1,5},{5,9},{9,13},{14,2},{2,6},{... | collective-permute-start | bytes 393224 | tf_op jit(solution)/shard_map/ppermute | solution.py:148
  31.0 2.0 %collective-permute-start.1 = (bf16[4,64,256]{2,1,0:T(8,128)(2,1)S(1)}, bf16[4,64,256]{2,1,0:T(8,128)(2,1)S(1)}, u32[]{:S(2)}, u32[]{:S(2)}) collective-permute-start(bf16[4,64,256]{2,1,0:T(8,128)(2,1)S(1)} %get-tuple-element.167), channel_id=1, source_target_pairs={{4,0},{8,4},{12,8},{0,12},{5,1},{9,5},{13,9},{1,13},{6,2},{10,6},{... | collective-permute-start | bytes 393224 | tf_op jit(solution)/shard_map/ppermute | solution.py:148
  33.2 4.2 %collective-permute-done = bf16[4,64,256]{2,1,0:T(8,128)(2,1)S(1)} collective-permute-done((bf16[4,64,256]{2,1,0:T(8,128)(2,1)S(1)}, bf16[4,64,256]{2,1,0:T(8,128)(2,1)S(1)}, u32[]{:S(2)}, u32[]{:S(2)}) %collective-permute-start) | collective-permute-done | bytes 131104 | tf_op jit(solution)/shard_map/ppermute | solution.py:148
  37.4 1.9 %collective-permute-done.1 = bf16[4,64,256]{2,1,0:T(8,128)(2,1)S(1)} collective-permute-done((bf16[4,64,256]{2,1,0:T(8,128)(2,1)S(1)}, bf16[4,64,256]{2,1,0:T(8,128)(2,1)S(1)}, u32[]{:S(2)}, u32[]{:S(2)}) %collective-permute-start.1) | collective-permute-done | bytes 131104 | tf_op jit(solution)/shard_map/ppermute | solution.py:148
  41.0 1.0 %convolution_add_fusion.7.out_weight = f32[128,128]{1,0:T(8,128)} fusion(f32[128,128]{1,0:T(8,128)S(1)} %get-tuple-element.79, bf16[768,128]{1,0:T(8,128)(2,1)S(1)} %get-tuple-element.174, bf16[768,128]{1,0:T(8,128)(2,1)S(1)} %bitcast.81, bf16[768]{0:T(1024)(128)(2,1)S(1)} %reshape.150), kind=kOutput, calls=%fused_computation.62 | convolution fusion | flops 25280512 | bytes 525824 | tf_op jit(solution)/shard_map/dot_general | solution.py:175
  42.0 1.1 %convolution_add_fusion.6.in_weight = f32[256,128]{1,0:T(8,128)} fusion(f32[256,128]{1,0:T(8,128)S(1)} %get-tuple-element.77, bf16[768,256]{1,0:T(8,128)(2,1)S(1)} %bitcast.78, bf16[768,128]{1,0:T(8,128)(2,1)S(1)} %get-tuple-element.177, bf16[768]{0:T(1024)(128)(2,1)S(1)} %reshape.150), kind=kOutput, calls=%fused_computation.61 | convolution fusion | flops 50462720 | bytes 853504 | tf_op jit(solution)/shard_map/dot_general | solution.py:173
  43.6 15.6 %shard_map.136 = (f32[256,128]{1,0:T(8,128)}, f32[1,128]{1,0:T(1,128)}, f32[128,128]{1,0:T(8,128)}, f32[1,128]{1,0:T(1,128)}) custom-call(f32[256,128]{1,0:T(8,128)} %convolution_add_fusion.6.in_weight, f32[1,128]{1,0:T(1,128)} %get-tuple-element.179.in_bias, f32[128,128]{1,0:T(8,128)} %convolution_add_fusion.7.out_weight, f32[1,128]{1,0:T(1,128)} %get-tuple-element.178.out_bias), custom_call_target="tpu_custom_call" | custom-call | tf_op jit(solution)/shard_map/pallas_call | solution.py:120
  59.4 1.1 %fusion.39 = f32[1024,256]{1,0:T(8,128)S(1)} fusion(f32[1024,256]{1,0:T(8,128)S(1)} %get-tuple-element.76, bf16[768,256]{1,0:T(8,128)(2,1)S(1)} %bitcast.82, s32[768]{0:T(1024)S(1)} %copy-done.8), kind=kOutput, calls=%fused_computation.52 | convolution fusion | flops 403701760 | bytes 2493440 | tf_op jit(solution)/shard_map/dot_general | solution.py:193
  60.6 0.9 %fusion.44 = (bf16[1024,128]{1,0:T(8,128)(2,1)}, bf16[1024,128]{1,0:T(8,128)(2,1)}) fusion(f32[1024,256]{1,0:T(8,128)S(1)} %fusion.39, bf16[1024,128]{1,0:T(8,128)(2,1)S(1)} %copy-done.3, bf16[1024,128]{1,0:T(8,128)(2,1)S(1)} %copy-done.2), kind=kLoop, calls=%fused_computation.64 | loop fusion | flops 786432 | bytes 2097152 | tf_op jit(solution)/shard_map/convert_element_type | solution.py:295
  61.5 0.7 %copy.43 = f32[256,128]{1,0:T(8,128)} copy(f32[256,128]{1,0:T(8,128)S(1)} %copy-done.4) | data formatting | bytes 262144
  62.7 0.6 copy.45
  (82 shorter events, 10.2 us)
Async XLA Ops:
  0.6 2.0 %copy-start.8 = (s32[768]{0:T(1024)S(1)}, s32[768]{0:T(1024)}, u32[]{:S(2)}) copy-start(s32[768]{0:T(1024)} %param.14) | copy-start | bytes 9220
  3.4 5.1 %copy-start.7 = (s32[12]{0:T(128)S(1)}, s32[12]{0:T(128)}, u32[]{:S(2)}) copy-start(s32[12]{0:T(128)} %param.15) | copy-start | bytes 148
  3.4 5.1 %copy-start = (bf16[256,128]{1,0:T(8,128)(2,1)S(1)}, bf16[256,128]{1,0:T(8,128)(2,1)}, u32[]{:S(2)}) copy-start(bf16[256,128]{1,0:T(8,128)(2,1)} %param.16) | copy-start | bytes 196612
  3.4 5.1 %copy-start.1 = (bf16[128,128]{1,0:T(8,128)(2,1)S(1)}, bf16[128,128]{1,0:T(8,128)(2,1)}, u32[]{:S(2)}) copy-start(bf16[128,128]{1,0:T(8,128)(2,1)} %param.18) | copy-start | bytes 98308
  3.4 5.1 %copy-start.6 = (f32[128]{0:T(128)S(1)}, f32[128]{0:T(128)}, u32[]{:S(2)}) copy-start(f32[128]{0:T(128)} %param.19) | copy-start | bytes 1540
  3.4 5.1 %copy-start.9 = (f32[128]{0:T(128)S(1)}, f32[128]{0:T(128)}, u32[]{:S(2)}) copy-start(f32[128]{0:T(128)} %param.17) | copy-start | bytes 1540
  4.2 24.3 %all-to-all-start = ((bf16[3,4,64,256]{3,2,0,1:T(8,128)(2,1)}), bf16[3,4,64,256]{3,2,0,1:T(8,128)(2,1)S(1)}, u32[]{:S(2)}, u32[]{:S(2)}) async-start(bf16[3,4,64,256]{3,2,0,1:T(8,128)(2,1)} %copy.15), calls=%async_computation | async-start | bytes 786432 | tf_op jit(solution)/shard_map/all_to_all | solution.py:199
  28.6 8.8 %collective-permute-start = (bf16[4,64,256]{2,1,0:T(8,128)(2,1)S(1)}, bf16[4,64,256]{2,1,0:T(8,128)(2,1)S(1)}, u32[]{:S(2)}, u32[]{:S(2)}) collective-permute-start(bf16[4,64,256]{2,1,0:T(8,128)(2,1)S(1)} %get-tuple-element.166), channel_id=1, source_target_pairs={{12,0},{0,4},{4,8},{8,12},{13,1},{1,5},{5,9},{9,13},{14,2},{2,6},{... | collective-permute-start | bytes 393224 | tf_op jit(solution)/shard_map/ppermute | solution.py:148
  31.0 8.3 %collective-permute-start.1 = (bf16[4,64,256]{2,1,0:T(8,128)(2,1)S(1)}, bf16[4,64,256]{2,1,0:T(8,128)(2,1)S(1)}, u32[]{:S(2)}, u32[]{:S(2)}) collective-permute-start(bf16[4,64,256]{2,1,0:T(8,128)(2,1)S(1)} %get-tuple-element.167), channel_id=1, source_target_pairs={{4,0},{8,4},{12,8},{0,12},{5,1},{9,5},{13,9},{1,13},{6,2},{10,6},{... | collective-permute-start | bytes 393224 | tf_op jit(solution)/shard_map/ppermute | solution.py:148
  59.4 1.2 %copy-start.2 = (bf16[1024,128]{1,0:T(8,128)(2,1)S(1)}, bf16[1024,128]{1,0:T(8,128)(2,1)}, u32[]{:S(2)}) copy-start(bf16[1024,128]{1,0:T(8,128)(2,1)} %param.11) | copy-start | bytes 786436
  59.4 1.2 %copy-start.3 = (bf16[1024,128]{1,0:T(8,128)(2,1)S(1)}, bf16[1024,128]{1,0:T(8,128)(2,1)}, u32[]{:S(2)}) copy-start(bf16[1024,128]{1,0:T(8,128)(2,1)} %param.12) | copy-start | bytes 786436
  60.6 0.9 %copy-start.4 = (f32[256,128]{1,0:T(8,128)S(1)}, f32[256,128]{1,0:T(8,128)}, u32[]{:S(2)}) copy-start(f32[256,128]{1,0:T(8,128)} %get-tuple-element.330) | copy-start | bytes 393220
  60.6 1.6 %copy-start.11 = (f32[1,128]{1,0:T(1,128)S(1)}, f32[1,128]{1,0:T(1,128)}, u32[]{:S(2)}) copy-start(f32[1,128]{1,0:T(1,128)} %get-tuple-element.82) | copy-start | bytes 1540
  60.6 2.1 %copy-start.5 = (f32[128,128]{1,0:T(8,128)S(1)}, f32[128,128]{1,0:T(8,128)}, u32[]{:S(2)}) copy-start(f32[128,128]{1,0:T(8,128)} %get-tuple-element.332) | copy-start | bytes 196612
  60.6 2.7 %copy-start.10 = (f32[1,128]{1,0:T(1,128)S(1)}, f32[1,128]{1,0:T(1,128)}, u32[]{:S(2)}) copy-start(f32[1,128]{1,0:T(1,128)} %get-tuple-element.84) | copy-start | bytes 1540

commit v2 on v0

v2 whole, which is shorter than its diff:
```python
import functools

import jax
import jax.numpy as jnp
from jax import lax
from jax.experimental import pallas as pl
from jax.experimental.pallas import tpu as pltpu
from jax.sharding import PartitionSpec as P

MESH = pl.DeviceIdType.MESH


def round_up(value, step):
    return -(-value // step) * step


def device_at(rank, subparts):
    return {"region": rank // subparts, "sub": lax.rem(rank, subparts)}


def high_low(value):
    high = value.astype(jnp.bfloat16).astype(jnp.float32)
    return high, value - high


def exchange(me, total, subparts, source, target, send_sem, recv_sem):
    def copy_of(step):
        peer = lax.rem(me + step, total)
        return pltpu.make_async_remote_copy(
            src_ref=source(peer),
            dst_ref=target(step),
            send_sem=send_sem.at[step],
            recv_sem=recv_sem.at[step],
            device_id=device_at(peer, subparts),
            device_id_type=MESH,
        )

    def begin(step, unused):
        copy_of(step).start()
        return unused

    def finish(step, unused):
        copy_of(step).wait()
        return unused

    return (
        lambda: lax.fori_loop(1, total, begin, 0),
        lambda: lax.fori_loop(1, total, finish, 0),
    )


def normalized(gradient):
    return gradient / jnp.sqrt(jnp.mean(gradient * gradient) + 1e-06)


def dot(left, right, left_axis=1, right_axis=0):
    return lax.dot_general(
        left, right, (((left_axis,), (right_axis,)), ((), ())), preferred_element_type=jnp.float32
    )


def one_hot(match):
    return jnp.where(match, 1.0, 0.0).astype(jnp.bfloat16)


def edge_by_cell(cell_row, cell_count):
    rows = cell_row.shape[1]
    spread = jnp.transpose(jnp.broadcast_to(cell_row, (128, rows)))
    lane = lax.broadcasted_iota(jnp.int32, (rows, 128), 1)
    return jnp.concatenate(
        [one_hot(spread == lane + start) for start in range(0, cell_count, 128)], axis=1
    )


def cell_by_edge(cell_row, cell_count):
    cell = lax.broadcasted_iota(jnp.int32, (cell_count, cell_row.shape[1]), 0)
    return one_hot(cell == cell_row)


def edge_network(head_rows, tail_rows, live, in_weight, in_bias, out_weight, out_bias):
    channels = out_weight.shape[1]
    inputs = jnp.concatenate([head_rows[:, :channels], tail_rows[:, :channels]], axis=1)
    before = dot(inputs, in_weight) + in_bias
    logistic = 1.0 / (1.0 + jnp.exp(-before))
    hidden = (before * logistic).astype(jnp.bfloat16)
    flux = (dot(hidden, out_weight) + out_bias).astype(jnp.bfloat16)
    d_flux = head_rows[:, channels:].astype(jnp.float32) - tail_rows[:, channels:].astype(jnp.float32)
    if live is not None:
        d_flux = d_flux * live
    d_flux = d_flux.astype(jnp.bfloat16)
    d_hidden = dot(d_flux, out_weight, 1, 1)
    d_before = (d_hidden * logistic * (1.0 + before * (1.0 - logistic))).astype(jnp.bfloat16)
    d_inputs = dot(d_before, in_weight, 1, 1).astype(jnp.bfloat16)
    return inputs, hidden, flux, d_flux, d_before, d_inputs


def layer_kernel(
    regions, subparts, chunk, block,
    latents, cotangent, edges, cut_cells, pair_count, in_weight, in_bias, out_weight, out_bias,
    new_latents, latent_grad, in_weight_out, in_bias_out, out_weight_out, out_bias_out,
    both, own, incoming, heads, tails, live_rows, lead_rows, pieces, cut_pieces, accum,
    terms, bias_terms, sent, landed, gathered,
    cut_send, cut_recv, send_a, recv_a, send_b, recv_b,
):
    total = regions * subparts
    region = lax.axis_index("region")
    subpart = lax.axis_index("sub")
    me = region * subparts + subpart
    cell_count, channels = latents.shape
    wide = in_weight.shape[0]
    narrow = out_weight.shape[0]
    slot_rows = sent.shape[1]
    lists, slots = own.shape[0], own.shape[1]
    blocks = edges.shape[1] // block
    f32 = jnp.float32

    barrier = pltpu.get_barrier_semaphore()

    def greet(step, unused):
        peer = lax.rem(me + step, total)
        pl.semaphore_signal(barrier, inc=1, device_id=device_at(peer, subparts), device_id_type=MESH)
        return unused

    lax.fori_loop(1, total, greet, 0)

    both[:, :channels] = latents[...]
    both[:, channels:] = cotangent[...]
    terms[...] = jnp.zeros(terms.shape, f32)
    bias_terms[...] = jnp.zeros(bias_terms.shape, f32)
    group = subparts * slots

    def pick_cut(offset, unused):
        at = pl.multiple_of(offset * group, 128)
        table = edge_by_cell(cut_cells[:, pl.ds(at, group)], cell_count)
        rows = dot(table, both[...]).astype(jnp.bfloat16)
        own[pl.ds(offset * subparts, subparts)] = rows.reshape(subparts, slots, 2 * channels)
        return unused

    lax.fori_loop(0, 3, pick_cut, 0)
    incoming[subparts + subpart] = jnp.zeros((slots, 2 * channels), jnp.bfloat16)
    pl.semaphore_wait(barrier, total - 1)

    def cut_copy(index):
        offset = index // subparts
        other = lax.rem(index, subparts)
        there = (2 - offset) * subparts + subpart
        return pltpu.make_async_remote_copy(
            src_ref=own.at[index],
            dst_ref=incoming.at[there],
            send_sem=cut_send.at[index],
            recv_sem=cut_recv.at[there],
            device_id={"region": lax.rem(region + offset + regions - 1, regions), "sub": other},
            device_id_type=MESH,
        )

    def landed_copy(index):
        return pltpu.make_async_remote_copy(
            src_ref=own.at[index],
            dst_ref=incoming.at[index],
            send_sem=cut_send.at[index],
            recv_sem=cut_recv.at[index],
            device_id={
                "region": lax.rem(region + index // subparts + regions - 1, regions),
                "sub": lax.rem(index, subparts),
            },
            device_id_type=MESH,
        )

    def send_cut(index, unused):
        @pl.when(index != subparts + subpart)
        def begin():
            cut_copy(index).start()

        return unused

    lax.fori_loop(0, lists, send_cut, 0)

    def add_terms(inputs, hidden, d_before, d_flux):
        terms[0:wide] += dot(inputs, d_before, 0, 0)
        terms[wide : wide + narrow] += dot(hidden, d_flux, 0, 0)
        bias_terms[0:1] += jnp.sum(d_before.astype(f32), axis=0, keepdims=True)
        bias_terms[1:2] += jnp.sum(d_flux.astype(f32), axis=0, keepdims=True)

    def interior(index, unused):
        at = pl.multiple_of(index * block, 128)
        head_rows = dot(edge_by_cell(edges[0:1, pl.ds(at, block)], cell_count), both[...])
        tail_rows = dot(edge_by_cell(edges[1:2, pl.ds(at, block)], cell_count), both[...])
        inputs, hidden, flux, d_flux, d_before, d_inputs = edge_network(
            head_rows.astype(jnp.bfloat16), tail_rows.astype(jnp.bfloat16), None,
            in_weight[...], in_bias[...], out_weight[...], out_bias[...],
        )
        pieces[index, 0:block, :channels] = flux
        pieces[index, 0:block, channels:] = d_inputs[:, :channels]
        pieces[index, block:, :channels] = -flux
        pieces[index, block:, channels:] = d_inputs[:, channels:]
        add_terms(inputs, hidden, d_before, d_flux)
        return unused

    lax.fori_loop(0, blocks, interior, 0)

    def arrange(index, unused):
        @pl.when(index != subparts + subpart)
        def finish():
            landed_copy(index).wait_recv()

        offset = index // subparts
        peer = lax.rem(region + offset + regions - 1, regions) * subparts + lax.rem(index, subparts)
        lead = jnp.where(me < peer, 1.0, 0.0)
        at = pl.multiple_of(index * slots, 16)
        mask = jnp.full((slots, 2 * channels), lead, f32) > 0.5
        mine, other = own[index].astype(f32), incoming[index].astype(f32)
        heads[pl.ds(at, slots)] = jnp.where(mask, mine, other).astype(jnp.bfloat16)
        tails[pl.ds(at, slots)] = jnp.where(mask, other, mine).astype(jnp.bfloat16)
        slot = lax.broadcasted_iota(jnp.int32, (slots, channels), 0)
        live_rows[pl.ds(at, slots)] = jnp.where(slot < pair_count[index], 1.0, 0.0)
        lead_rows[pl.ds(at, slots)] = jnp.full((slots, channels), lead, f32)
        return unused

    lax.fori_loop(0, lists, arrange, 0)

    def cut(offset, unused):
        at = pl.multiple_of(offset * group, 128)
        rows = pl.ds(at, group)
        live, lead = live_rows[rows], lead_rows[rows]
        inputs, hidden, flux, d_flux, d_before, d_inputs = edge_network(
            heads[rows], tails[rows], live,
            in_weight[...], in_bias[...], out_weight[...], out_bias[...],
        )
        owned = live * lead
        sign = live * (2.0 * lead - 1.0)
        cut_pieces[rows, :channels] = (flux.astype(f32) * sign).astype(jnp.bfloat16)
        spread = d_inputs.astype(f32)
        cut_pieces[rows, channels:] = jnp.where(
            lead > 0.5, spread[:, :channels], spread[:, channels:]
        ).astype(jnp.bfloat16)
        add_terms(
            inputs, hidden,
            (d_before.astype(f32) * owned).astype(jnp.bfloat16),
            (d_flux.astype(f32) * owned).astype(jnp.bfloat16),
        )
        return unused

    lax.fori_loop(0, 3, cut, 0)

    bias_rows = jnp.concatenate(
        [*high_low(bias_terms[0:1]), *high_low(bias_terms[1:2]),
         jnp.zeros((slot_rows - chunk - 4, channels), f32)], axis=0
    )

    def fill(rank, unused):
        part = terms[pl.ds(pl.multiple_of(rank * chunk, 8), chunk)]
        sent[rank] = jnp.concatenate([part, bias_rows], axis=0).astype(jnp.bfloat16)
        return unused

    lax.fori_loop(0, total, fill, 0)
    begin_a, finish_a = exchange(
        me, total, subparts, lambda peer: sent.at[peer], lambda step: landed.at[step], send_a, recv_a
    )
    begin_a()
    landed[0] = sent[me]

    def spread_block(index, unused):
        at = pl.multiple_of(index * block, 128)
        head_table = cell_by_edge(edges[0:1, pl.ds(at, block)], cell_count)
        tail_table = cell_by_edge(edges[1:2, pl.ds(at, block)], cell_count)
        accum[...] += dot(head_table, pieces[index, 0:block]) + dot(tail_table, pieces[index, block:])
        return unused

    accum[...] = dot(cell_by_edge(cut_cells[...], cell_count), cut_pieces[...])
    first = blocks // 2
    lax.fori_loop(0, first, spread_block, 0)
    finish_a()
    owned_sum = jnp.sum(landed[...].astype(f32), axis=0)
    gathered[me] = owned_sum.astype(jnp.bfloat16)
    begin_b, finish_b = exchange(
        me, total, subparts, lambda peer: gathered.at[me], lambda step: gathered.at[me], send_b, recv_b
    )
    begin_b()
    lax.fori_loop(first, blocks, spread_block, 0)
    in_bias_out[...] = normalized(owned_sum[chunk : chunk + 1] + owned_sum[chunk + 1 : chunk + 2])
    out_bias_out[...] = normalized(owned_sum[chunk + 2 : chunk + 3] + owned_sum[chunk + 3 : chunk + 4])
    new_latents[...] = (latents[...].astype(f32) + accum[:, :channels]).astype(jnp.bfloat16)
    latent_grad[...] = (cotangent[...].astype(f32) + accum[:, channels:]).astype(jnp.bfloat16)

    def sent_cut(index, unused):
        @pl.when(index != subparts + subpart)
        def finish():
            landed_copy(index).wait_send()

        return unused

    lax.fori_loop(0, lists, sent_cut, 0)
    finish_b()
    everything = gathered[...].astype(f32)[:, :chunk].reshape(total * chunk, channels)
    in_weight_out[...] = normalized(everything[:wide])
    out_weight_out[...] = normalized(everything[wide : wide + narrow])


def local(
    latents, cotangent, inner_edges, cut_cells, pair_count, in_weight, in_bias, out_weight, out_bias
):
    regions = lax.axis_size("region")
    subparts = lax.axis_size("sub")
    total = regions * subparts
    cell_count, channels = latents.shape
    edge_total = inner_edges.shape[1]
    wide, hidden = in_weight.shape
    narrow = out_weight.shape[0]
    lists = pair_count.shape[0]
    slots = cut_cells.shape[0] // lists
    cut_total = lists * slots
    block = 1024
    blocks = edge_total // block
    chunk = round_up(-(-(wide + narrow) // total), 8)
    slot_rows = round_up(chunk + 4, 16)
    vmem = pl.BlockSpec(memory_space=pltpu.VMEM)
    smem = pl.BlockSpec(memory_space=pltpu.SMEM)
    f32, bf16 = jnp.float32, jnp.bfloat16
    dma = pltpu.SemaphoreType.DMA
    a, b, c, d, e, f = pl.pallas_call(
        functools.partial(layer_kernel, regions, subparts, chunk, block),
        out_shape=[
            jax.ShapeDtypeStruct((cell_count, channels), bf16),
            jax.ShapeDtypeStruct((cell_count, channels), bf16),
            jax.ShapeDtypeStruct((wide, hidden), f32),
            jax.ShapeDtypeStruct((1, hidden), f32),
            jax.ShapeDtypeStruct((narrow, channels), f32),
            jax.ShapeDtypeStruct((1, channels), f32),
        ],
        in_specs=[vmem] * 4 + [smem] + [vmem] * 4,
        out_specs=[vmem] * 6,
        scratch_shapes=[
            pltpu.VMEM((cell_count, 2 * channels), bf16),
            pltpu.VMEM((lists, slots, 2 * channels), bf16),
            pltpu.VMEM((lists, slots, 2 * channels), bf16),
            pltpu.VMEM((cut_total, 2 * channels), bf16),
            pltpu.VMEM((cut_total, 2 * channels), bf16),
            pltpu.VMEM((cut_total, channels), f32),
            pltpu.VMEM((cut_total, channels), f32),
            pltpu.VMEM((blocks, 2 * block, 2 * channels), bf16),
            pltpu.VMEM((cut_total, 2 * channels), bf16),
            pltpu.VMEM((cell_count, 2 * channels), f32),
            pltpu.VMEM((max(total * chunk, wide + narrow), channels), f32),
            pltpu.VMEM((8, channels), f32),
            pltpu.VMEM((total, slot_rows, channels), bf16),
            pltpu.VMEM((total, slot_rows, channels), bf16),
            pltpu.VMEM((total, slot_rows, channels), bf16),
            dma((lists,)),
            dma((lists,)),
            dma((total,)),
            dma((total,)),
            dma((total,)),
            dma((total,)),
        ],
        compiler_params=pltpu.CompilerParams(
            collective_id=0, has_side_effects=True, vmem_limit_bytes=48 * 1024 * 1024
        ),
    )(
        latents, cotangent, inner_edges, cut_cells[None], pair_count,
        in_weight, in_bias[None], out_weight, out_bias[None],
    )
    return a, b, c, d[0], e, f[0]


def solution(mesh):
    placed = (
        P(("groups", "region", "sub"), None),
        P(("groups", "region", "sub"), None),
        P(None, ("groups", "region", "sub")),
        P(("groups", "region", "sub")),
        P(("groups", "region", "sub")),
        P(),
        P(),
        P(),
        P(),
    )
    return jax.shard_map(
        local,
        mesh=mesh,
        in_specs=placed,
        out_specs=(
            P(("groups", "region", "sub"), None),
            P(("groups", "region", "sub"), None),
            P("groups", None),
            P("groups"),
            P("groups", None),
            P("groups"),
        ),
        check_vma=False,
    )
```

time: 189 us -> 36.7 us (0.19)
  waiting for transfers between devices: 92.9 us -> 0 us
  blocking collectives: 31.7 us -> 0 us
  Pallas kernels: 0 us -> 26.9 us
  matrix products: 21.5 us -> 0 us
  between operations: 17 us -> 0.68 us
  other arithmetic: 10.1 us -> 0 us
  starting transfers between devices: 8.73 us -> 0 us
  local copies, waits for them, and re-layouts: 5.61 us -> 8.66 us
    psum x1 -> x0, waiting for transfers between devices: 86.8 us -> none  [local(): lax.psum((in_weight_sum, in_bias_sum, out_weight_sum, out_bias_sum), ('re...]
    psum x1 -> x0, blocking collectives: 31.7 us -> none  [local(): lax.psum((in_weight_sum, in_bias_sum, out_weight_sum, out_bias_sum), ('re...]
    pallas_call x0 -> x1, Pallas kernels: none -> 26.9 us  [local(): pl.pallas_call(functools.partial(layer_kernel, regions, subparts, chunk,...]
    dot_general x38 -> x0, matrix products: 21.5 us -> none  [the longest x7 6.95 us: spread_rows(): lax.dot_general(table, pieces, (((0,), (0,)), ((), ())), preferred_elemen...]
    unnamed x17 -> x22, local copies, waits for them, and re-layouts: 1.05 us -> 7.95 us
    ppermute x2 -> x0, waiting for transfers between devices: 6.06 us -> none  [from_behind(): return lax.ppermute(block, axis, route)]
    ppermute x2 -> x0, starting transfers between devices: 4.52 us -> none  [from_behind(): return lax.ppermute(block, axis, route)]
    reduce_sum x7 -> x0, other arithmetic: 4.48 us -> none  [the longest x3 3.61 us: normalized(): return gradient / jnp.sqrt(jnp.mean(gradient * gradient) + 1e-06)]
  transfers between devices with their start and end apart: 4 -> 0, of which waited for: 3 -> 0; matrix products, arithmetic and copies ran while one was open for 11% -> 0% of each run, Pallas kernels for 0% -> 0%
where the time goes in v2:
time: 36.7 us; the launch traced here: 36.3 us
  Pallas kernels  26.9 us (73%)
  local copies, waits for them, and re-layouts  8.66 us (24%)
  between operations  0.68 us (2%)
    pallas_call x1, Pallas kernels, local(): pl.pallas_call(functools.partial(layer_kernel, regions, subparts, chunk,...  26.9 us
    unnamed x22, local copies, waits for them, and re-layouts  7.95 us

profile of v2, /device:TPU:0, one launch (start us, length us, event | category | flops | bytes accessed | tf_op | source)
XLA Modules:
  0.0 36.3 jit_solution(16258642318313712007)
XLA Ops:
  0.6 0.0 copy-start.5
  0.6 0.0 copy-start.6
  0.7 0.0 copy-start.7
  0.7 0.7 %broadcast_in_dim.9.cut_cells = s32[1,768]{1,0:T(1,128)S(1)} reshape(s32[768]{0:T(1024)} %param.12) | data formatting | bytes 6144 | tf_op jit(solution)/shard_map/broadcast_in_dim | solution.py:359
  1.4 0.0 copy-done.5
  1.4 0.0 copy-done.6
  1.4 0.0 copy-done.7
  1.4 0.0 copy-start
  1.4 0.9 %copy-done = bf16[1024,128]{1,0:T(8,128)(2,1)S(1)} copy-done((bf16[1024,128]{1,0:T(8,128)(2,1)S(1)}, bf16[1024,128]{1,0:T(8,128)(2,1)}, u32[]{:S(2)}) %copy-start) | copy-done | bytes 262168
  2.3 0.0 copy-start.1
  2.3 0.9 %copy-done.1 = bf16[1024,128]{1,0:T(8,128)(2,1)S(1)} copy-done((bf16[1024,128]{1,0:T(8,128)(2,1)S(1)}, bf16[1024,128]{1,0:T(8,128)(2,1)}, u32[]{:S(2)}) %copy-start.1) | copy-done | bytes 262168
  3.3 0.0 copy-start.2
  3.3 0.8 %copy-done.2 = bf16[256,128]{1,0:T(8,128)(2,1)S(1)} copy-done((bf16[256,128]{1,0:T(8,128)(2,1)S(1)}, bf16[256,128]{1,0:T(8,128)(2,1)}, u32[]{:S(2)}) %copy-start.2) | copy-done | bytes 65560
  4.1 0.0 copy-start.3
  4.1 0.8 %copy-done.3 = bf16[128,128]{1,0:T(8,128)(2,1)S(1)} copy-done((bf16[128,128]{1,0:T(8,128)(2,1)S(1)}, bf16[128,128]{1,0:T(8,128)(2,1)}, u32[]{:S(2)}) %copy-start.3) | copy-done | bytes 32792
  4.9 0.0 copy-start.4
  4.9 0.7 %copy-done.4 = s32[2,3072]{1,0:T(2,128)S(1)} copy-done((s32[2,3072]{1,0:T(2,128)S(1)}, s32[2,3072]{1,0:T(2,128)}, u32[]{:S(2)}) %copy-start.4) | copy-done | bytes 24600
  5.6 26.9 %shard_map.136 = (bf16[1024,128]{1,0:T(8,128)(2,1)S(1)}, bf16[1024,128]{1,0:T(8,128)(2,1)S(1)}, f32[256,128]{1,0:T(8,128)S(1)}, f32[1,128]{1,0:T(1,128)S(1)}, f3...) custom-call(bf16[1024,128]{1,0:T(8,128)(2,1)S(1)} %copy-done, bf16[1024,128]{1,0:T(8,128)(2,1)S(1)} %copy-done.1, ...), custom_call_target="tpu_custom_call" | custom-call | tf_op jit(solution)/shard_map/pallas_call | solution.py:320
  32.6 0.7 %copy.21 = bf16[1024,128]{1,0:T(8,128)(2,1)} copy(bf16[1024,128]{1,0:T(8,128)(2,1)S(1)} %get-tuple-element.24) | data formatting | bytes 524288
  33.3 0.7 %copy.22 = bf16[1024,128]{1,0:T(8,128)(2,1)} copy(bf16[1024,128]{1,0:T(8,128)(2,1)S(1)} %get-tuple-element.25) | data formatting | bytes 524288
  34.0 0.7 %copy.23 = f32[256,128]{1,0:T(8,128)} copy(f32[256,128]{1,0:T(8,128)S(1)} %get-tuple-element.26) | data formatting | bytes 262144
  34.6 0.5 %copy.24 = f32[128]{0:T(128)} copy(f32[128]{0:T(128)S(1)} %bitcast.7) | data formatting | bytes 1024
  35.1 0.6 %copy.25 = f32[128,128]{1,0:T(8,128)} copy(f32[128,128]{1,0:T(8,128)S(1)} %get-tuple-element.28) | data formatting | bytes 131072
  35.8 0.5 %copy.26 = f32[128]{0:T(128)} copy(f32[128]{0:T(128)S(1)} %bitcast.6) | data formatting | bytes 1024
Async XLA Ops:
  0.6 0.7 %copy-start.5 = (s32[12]{0:T(128)S(1)}, s32[12]{0:T(128)}, u32[]{:S(2)}) copy-start(s32[12]{0:T(128)} %pair_count.1) | copy-start | bytes 148
  0.6 0.7 %copy-start.6 = (f32[128]{0:T(128)S(1)}, f32[128]{0:T(128)}, u32[]{:S(2)}) copy-start(f32[128]{0:T(128)} %param.15) | copy-start | bytes 1540
  0.7 0.7 %copy-start.7 = (f32[128]{0:T(128)S(1)}, f32[128]{0:T(128)}, u32[]{:S(2)}) copy-start(f32[128]{0:T(128)} %param.17) | copy-start | bytes 1540
  1.4 1.0 %copy-start = (bf16[1024,128]{1,0:T(8,128)(2,1)S(1)}, bf16[1024,128]{1,0:T(8,128)(2,1)}, u32[]{:S(2)}) copy-start(bf16[1024,128]{1,0:T(8,128)(2,1)} %latents.1) | copy-start | bytes 786436
  2.3 0.9 %copy-start.1 = (bf16[1024,128]{1,0:T(8,128)(2,1)S(1)}, bf16[1024,128]{1,0:T(8,128)(2,1)}, u32[]{:S(2)}) copy-start(bf16[1024,128]{1,0:T(8,128)(2,1)} %cotangent.1) | copy-start | bytes 786436
  3.3 0.8 %copy-start.2 = (bf16[256,128]{1,0:T(8,128)(2,1)S(1)}, bf16[256,128]{1,0:T(8,128)(2,1)}, u32[]{:S(2)}) copy-start(bf16[256,128]{1,0:T(8,128)(2,1)} %in_weight.1) | copy-start | bytes 196612
  4.1 0.8 %copy-start.3 = (bf16[128,128]{1,0:T(8,128)(2,1)S(1)}, bf16[128,128]{1,0:T(8,128)(2,1)}, u32[]{:S(2)}) copy-start(bf16[128,128]{1,0:T(8,128)(2,1)} %out_weight.1) | copy-start | bytes 98308
  4.9 0.7 %copy-start.4 = (s32[2,3072]{1,0:T(2,128)S(1)}, s32[2,3072]{1,0:T(2,128)}, u32[]{:S(2)}) copy-start(s32[2,3072]{1,0:T(2,128)} %edges.1) | copy-start | bytes 73732

commit v3 on v2

--- a/solution.py
+++ b/solution.py
@@ -59,22 +59,28 @@
     )
 
 
-def one_hot(match):
-    return jnp.where(match, 1.0, 0.0).astype(jnp.bfloat16)
-
-
 def edge_by_cell(cell_row, cell_count):
     rows = cell_row.shape[1]
     spread = jnp.transpose(jnp.broadcast_to(cell_row, (128, rows)))
     lane = lax.broadcasted_iota(jnp.int32, (rows, 128), 1)
+    low = jnp.where(spread & 127 == lane, 1.0, 0.0).astype(jnp.bfloat16)
+    high = (lax.shift_right_logical(spread, 7)).astype(jnp.float32).astype(jnp.bfloat16)
+    zero = jnp.zeros((rows, 128), jnp.bfloat16)
     return jnp.concatenate(
-        [one_hot(spread == lane + start) for start in range(0, cell_count, 128)], axis=1
+        [jnp.where(high == jnp.bfloat16(part), low, zero) for part in range(cell_count // 128)], axis=1
     )
 
 
 def cell_by_edge(cell_row, cell_count):
-    cell = lax.broadcasted_iota(jnp.int32, (cell_count, cell_row.shape[1]), 0)
-    return one_hot(cell == cell_row)
+    rows = cell_row.shape[1]
+    spread = jnp.broadcast_to(cell_row, (16, rows))
+    cell = lax.broadcasted_iota(jnp.int32, (16, rows), 0)
+    low = jnp.where(spread & 15 == cell, 1.0, 0.0).astype(jnp.bfloat16)
+    high = (lax.shift_right_logical(spread, 4)).astype(jnp.float32).astype(jnp.bfloat16)
+    zero = jnp.zeros((16, rows), jnp.bfloat16)
+    return jnp.concatenate(
+        [jnp.where(high == jnp.bfloat16(part), low, zero) for part in range(cell_count // 16)], axis=0
+    )
 
 
 def edge_network(head_rows, tail_rows, live, in_weight, in_bias, out_weight, out_bias):
@@ -96,8 +102,9 @@
 
 def layer_kernel(
     regions, subparts, chunk, block,
-    latents, cotangent, edges, cut_cells, pair_count, in_weight, in_bias, out_weight, out_bias,
+    latents_from, cotangent_from, edges_from, cut_flat, pair_count, in_weight_from, in_bias, out_weight_from, out_bias,
     new_latents, latent_grad, in_weight_out, in_bias_out, out_weight_out, out_bias_out,
+    latents, cotangent, edges, cut_cells, in_weight, out_weight, arrived,
     both, own, incoming, heads, tails, live_rows, lead_rows, pieces, cut_pieces, accum,
     terms, bias_terms, sent, landed, gathered,
     cut_send, cut_recv, send_a, recv_a, send_b, recv_b,
@@ -114,6 +121,20 @@
     blocks = edges.shape[1] // block
     f32 = jnp.float32
 
+    fetches = [
+        pltpu.make_async_copy(source, target, arrived.at[place])
+        for place, (source, target) in enumerate(
+            (
+                (latents_from, latents),
+                (cotangent_from, cotangent),
+                (edges_from, edges),
+                (in_weight_from, in_weight),
+                (out_weight_from, out_weight),
+            )
+        )
+    ]
+    for fetch in fetches:
+        fetch.start()
     barrier = pltpu.get_barrier_semaphore()
 
     def greet(step, unused):
@@ -123,6 +144,9 @@
 
     lax.fori_loop(1, total, greet, 0)
 
+    cut_cells[...] = cut_flat[...].reshape(1, -1)
+    for fetch in fetches:
+        fetch.wait()
     both[:, :channels] = latents[...]
     both[:, channels:] = cotangent[...]
     terms[...] = jnp.zeros(terms.shape, f32)
@@ -294,6 +318,18 @@
     everything = gathered[...].astype(f32)[:, :chunk].reshape(total * chunk, channels)
     in_weight_out[...] = normalized(everything[:wide])
     out_weight_out[...] = normalized(everything[wide : wide + narrow])
+
+
+def hand_on(*refs):
+    sources, targets, done = refs[:6], refs[6:12], refs[12]
+    copies = [
+        pltpu.make_async_copy(source, target, done.at[place])
+        for place, (source, target) in enumerate(zip(sources, targets))
+    ]
+    for copy in copies:
+        copy.start()
+    for copy in copies:
+        copy.wait()
 
 
 def local(
@@ -314,10 +350,11 @@
     chunk = round_up(-(-(wide + narrow) // total), 8)
     slot_rows = round_up(chunk + 4, 16)
     vmem = pl.BlockSpec(memory_space=pltpu.VMEM)
+    hbm = pl.BlockSpec(memory_space=pl.ANY)
     smem = pl.BlockSpec(memory_space=pltpu.SMEM)
     f32, bf16 = jnp.float32, jnp.bfloat16
     dma = pltpu.SemaphoreType.DMA
-    a, b, c, d, e, f = pl.pallas_call(
+    results = pl.pallas_call(
         functools.partial(layer_kernel, regions, subparts, chunk, block),
         out_shape=[
             jax.ShapeDtypeStruct((cell_count, channels), bf16),
@@ -327,9 +364,16 @@
             jax.ShapeDtypeStruct((narrow, channels), f32),
             jax.ShapeDtypeStruct((1, channels), f32),
         ],
-        in_specs=[vmem] * 4 + [smem] + [vmem] * 4,
+        in_specs=[hbm, hbm, hbm, vmem, smem, hbm, vmem, hbm, vmem],
         out_specs=[vmem] * 6,
         scratch_shapes=[
+            pltpu.VMEM((cell_count, channels), bf16),
+            pltpu.VMEM((cell_count, channels), bf16),
+            pltpu.VMEM((2, edge_total), jnp.int32),
+            pltpu.VMEM((1, cut_total), jnp.int32),
+            pltpu.VMEM((wide, hidden), bf16),
+            pltpu.VMEM((narrow, channels), bf16),
+            dma((5,)),
             pltpu.VMEM((cell_count, 2 * channels), bf16),
             pltpu.VMEM((lists, slots, 2 * channels), bf16),
             pltpu.VMEM((lists, slots, 2 * channels), bf16),
@@ -353,12 +397,20 @@
             dma((total,)),
         ],
         compiler_params=pltpu.CompilerParams(
-            collective_id=0, has_side_effects=True, vmem_limit_bytes=48 * 1024 * 1024
+            collective_id=0, has_side_effects=True, vmem_limit_bytes=60 * 1024 * 1024
         ),
     )(
-        latents, cotangent, inner_edges, cut_cells[None], pair_count,
+        latents, cotangent, inner_edges, cut_cells, pair_count,
         in_weight, in_bias[None], out_weight, out_bias[None],
     )
+    a, b, c, d, e, f = pl.pallas_call(
+        hand_on,
+        out_shape=[jax.ShapeDtypeStruct(result.shape, result.dtype) for result in results],
+        in_specs=[hbm] * 6,
+        out_specs=[hbm] * 6,
+        scratch_shapes=[dma((6,))],
+        compiler_params=pltpu.CompilerParams(vmem_limit_bytes=60 * 1024 * 1024),
+    )(*results)
     return a, b, c, d[0], e, f[0]
 
 

time: 36.7 us -> 51.7 us (1.41)
  Pallas kernels: 26.9 us -> 50.9 us
  local copies, waits for them, and re-layouts: 8.66 us -> 0 us
    pallas_call x0 -> x1, Pallas kernels: none -> 23 us  [local(): pl.pallas_call(hand_on, out_shape=[jax.ShapeDtypeStruct(result.shape, res...]
    unnamed x22 -> x0, local copies, waits for them, and re-layouts: 7.95 us -> none
    pallas_call x1, Pallas kernels: 26.9 us -> 27.9 us  [local(): pl.pallas_call(functools.partial(layer_kernel, regions, subparts, chunk,...]
    broadcast_in_dim x1 -> x0, local copies, waits for them, and re-layouts: 0.71 us -> none  [local(): cut_cells[None]]
where the time goes in v3:
time: 51.7 us; the launch traced here: 51.5 us
  Pallas kernels  50.9 us (98%)
  between operations  0.64 us (1%)
    pallas_call x1, Pallas kernels, local(): pl.pallas_call(functools.partial(layer_kernel, regions, subparts, chunk,...  27.9 us
    pallas_call x1, Pallas kernels, local(): pl.pallas_call(hand_on, out_shape=[jax.ShapeDtypeStruct(result.shape, res...  23 us

profile of v3, /device:TPU:0, one launch (start us, length us, event | category | flops | bytes accessed | tf_op | source)
XLA Modules:
  0.0 51.5 jit_solution(567063031290872062)
XLA Ops:
  0.6 27.9 %shard_map.136 = (bf16[1024,128]{1,0:T(8,128)(2,1)}, bf16[1024,128]{1,0:T(8,128)(2,1)}, f32[256,128]{1,0:T(8,128)}, f32[1,128]{1,0:T(1,128)}, f32[128,128]{1,0:T(8,128)}, /*index=5*/f32[1,128]{1,0:T(1,128)}) custom-call(bf16[1024,128]{1,0:T(8,128)(2,1)} %latents_from.1, bf16[1024,128]{1,0:T(8,128)(2,1)} %cotangent_from.1, s32[2,3072]{1,0:T(2,128)} %edges_from.1, ...), custom_call_target="tpu_custom_call" | custom-call | tf_op jit(solution)/shard_map/pallas_call | solution.py:357
  28.5 23.0 %shard_map.137 = (bf16[1024,128]{1,0:T(8,128)(2,1)}, bf16[1024,128]{1,0:T(8,128)(2,1)}, f32[256,128]{1,0:T(8,128)}, f32[1,128]{1,0:T(1,128)}, f32[128,128]{1,0:T(8,128)}, /*index=5*/f32[1,128]{1,0:T(1,128)}) custom-call(bf16[1024,128]{1,0:T(8,128)(2,1)} %get-tuple-element.18.refs_0_, bf16[1024,128]{1,0:T(8,128)(2,1)} %get-tuple-element.19.refs_1_, ...), custom_call_target="tpu_custom_call" | custom-call | tf_op jit(solution)/shard_map/pallas_call | solution.py:406

commit v4 on v3

--- a/solution.py
+++ b/solution.py
@@ -15,7 +15,7 @@
 
 
 def device_at(rank, subparts):
-    return {"region": rank // subparts, "sub": lax.rem(rank, subparts)}
+    return {"region": lax.div(rank, jnp.int32(subparts)), "sub": lax.rem(rank, subparts)}
 
 
 def high_low(value):
@@ -106,7 +106,7 @@
     new_latents, latent_grad, in_weight_out, in_bias_out, out_weight_out, out_bias_out,
     latents, cotangent, edges, cut_cells, in_weight, out_weight, arrived,
     both, own, incoming, heads, tails, live_rows, lead_rows, pieces, cut_pieces, accum,
-    terms, bias_terms, sent, landed, gathered,
+    terms, wide_terms, bias_terms, sent, landed, gathered,
     cut_send, cut_recv, send_a, recv_a, send_b, recv_b,
 ):
     total = regions * subparts
@@ -150,6 +150,7 @@
     both[:, :channels] = latents[...]
     both[:, channels:] = cotangent[...]
     terms[...] = jnp.zeros(terms.shape, f32)
+    wide_terms[...] = jnp.zeros(wide_terms.shape, f32)
     bias_terms[...] = jnp.zeros(bias_terms.shape, f32)
     group = subparts * slots
 
@@ -200,7 +201,7 @@
     lax.fori_loop(0, lists, send_cut, 0)
 
     def add_terms(inputs, hidden, d_before, d_flux):
-        terms[0:wide] += dot(inputs, d_before, 0, 0)
+        wide_terms[...] += dot(d_before, inputs, 0, 0)
         terms[wide : wide + narrow] += dot(hidden, d_flux, 0, 0)
         bias_terms[0:1] += jnp.sum(d_before.astype(f32), axis=0, keepdims=True)
         bias_terms[1:2] += jnp.sum(d_flux.astype(f32), axis=0, keepdims=True)
@@ -220,7 +221,7 @@
         add_terms(inputs, hidden, d_before, d_flux)
         return unused
 
-    lax.fori_loop(0, blocks, interior, 0)
+    lax.fori_loop(0, blocks, interior, 0, unroll=True)
 
     def arrange(index, unused):
         @pl.when(index != subparts + subpart)
@@ -266,6 +267,7 @@
 
     lax.fori_loop(0, 3, cut, 0)
 
+    terms[0:wide] = jnp.transpose(wide_terms[...])
     bias_rows = jnp.concatenate(
         [*high_low(bias_terms[0:1]), *high_low(bias_terms[1:2]),
          jnp.zeros((slot_rows - chunk - 4, channels), f32)], axis=0
@@ -300,7 +302,7 @@
         me, total, subparts, lambda peer: gathered.at[me], lambda step: gathered.at[me], send_b, recv_b
     )
     begin_b()
-    lax.fori_loop(first, blocks, spread_block, 0)
+    lax.fori_loop(first, blocks, spread_block, 0, unroll=True)
     in_bias_out[...] = normalized(owned_sum[chunk : chunk + 1] + owned_sum[chunk + 1 : chunk + 2])
     out_bias_out[...] = normalized(owned_sum[chunk + 2 : chunk + 3] + owned_sum[chunk + 3 : chunk + 4])
     new_latents[...] = (latents[...].astype(f32) + accum[:, :channels]).astype(jnp.bfloat16)
@@ -321,15 +323,23 @@
 
 
 def hand_on(*refs):
-    sources, targets, done = refs[:6], refs[6:12], refs[12]
-    copies = [
-        pltpu.make_async_copy(source, target, done.at[place])
-        for place, (source, target) in enumerate(zip(sources, targets))
+    sources, targets, held = refs[:6], refs[6:12], refs[12:18]
+    came, left = refs[18], refs[19]
+    fetches = [
+        pltpu.make_async_copy(source, target, came.at[place])
+        for place, (source, target) in enumerate(zip(sources, held))
     ]
-    for copy in copies:
-        copy.start()
-    for copy in copies:
-        copy.wait()
+    writes = [
+        pltpu.make_async_copy(source, target, left.at[place])
+        for place, (source, target) in enumerate(zip(held, targets))
+    ]
+    for fetch in fetches:
+        fetch.start()
+    for fetch, write in zip(fetches, writes):
+        fetch.wait()
+        write.start()
+    for write in writes:
+        write.wait()
 
 
 def local(
@@ -385,6 +395,7 @@
             pltpu.VMEM((cut_total, 2 * channels), bf16),
             pltpu.VMEM((cell_count, 2 * channels), f32),
             pltpu.VMEM((max(total * chunk, wide + narrow), channels), f32),
+            pltpu.VMEM((hidden, wide), f32),
             pltpu.VMEM((8, channels), f32),
             pltpu.VMEM((total, slot_rows, channels), bf16),
             pltpu.VMEM((total, slot_rows, channels), bf16),
@@ -408,7 +419,7 @@
         out_shape=[jax.ShapeDtypeStruct(result.shape, result.dtype) for result in results],
         in_specs=[hbm] * 6,
         out_specs=[hbm] * 6,
-        scratch_shapes=[dma((6,))],
+        scratch_shapes=[*(pltpu.VMEM(result.shape, result.dtype) for result in results), dma((6,)), dma((6,))],
         compiler_params=pltpu.CompilerParams(vmem_limit_bytes=60 * 1024 * 1024),
     )(*results)
     return a, b, c, d[0], e, f[0]

time: 51.7 us -> 30.7 us (0.59)
  Pallas kernels: 50.9 us -> 29.9 us
    pallas_call x1, Pallas kernels: 23 us -> 1.91 us  [local(): pl.pallas_call(hand_on, out_shape=[jax.ShapeDtypeStruct(result.shape, res...]
where the time goes in v4:
time: 30.7 us; the launch traced here: 30.5 us
  Pallas kernels  29.9 us (97%)
  between operations  0.64 us (2%)
    pallas_call x1, Pallas kernels, local(): pl.pallas_call(functools.partial(layer_kernel, regions, subparts, chunk,...  28 us
    pallas_call x1, Pallas kernels, local(): pl.pallas_call(hand_on, out_shape=[jax.ShapeDtypeStruct(result.shape, res...  1.91 us

profile of v4, /device:TPU:0, one launch (start us, length us, event | category | flops | bytes accessed | tf_op | source)
XLA Modules:
  0.0 30.5 jit_solution(17122396379396957704)
XLA Ops:
  0.6 28.0 %shard_map.136 = (bf16[1024,128]{1,0:T(8,128)(2,1)}, bf16[1024,128]{1,0:T(8,128)(2,1)}, f32[256,128]{1,0:T(8,128)}, f32[1,128]{1,0:T(1,128)}, f32[128,128]{1,0:T(8,128)}, /*index=5*/f32[1,128]{1,0:T(1,128)}) custom-call(bf16[1024,128]{1,0:T(8,128)(2,1)} %latents_from.1, bf16[1024,128]{1,0:T(8,128)(2,1)} %cotangent_from.1, s32[2,3072]{1,0:T(2,128)} %edges_from.1, ...), custom_call_target="tpu_custom_call" | custom-call | tf_op jit(solution)/shard_map/pallas_call | solution.py:367
  28.6 1.9 %shard_map.137 = (bf16[1024,128]{1,0:T(8,128)(2,1)}, bf16[1024,128]{1,0:T(8,128)(2,1)}, f32[256,128]{1,0:T(8,128)}, f32[1,128]{1,0:T(1,128)}, f32[128,128]{1,0:T(8,128)}, /*index=5*/f32[1,128]{1,0:T(1,128)}) custom-call(bf16[1024,128]{1,0:T(8,128)(2,1)} %get-tuple-element.18.refs_0_, bf16[1024,128]{1,0:T(8,128)(2,1)} %get-tuple-element.19.refs_1_, ...), custom_call_target="tpu_custom_call" | custom-call | tf_op jit(solution)/shard_map/pallas_call | solution.py:417

commit v5 on v4

--- a/solution.py
+++ b/solution.py
@@ -152,16 +152,10 @@
     terms[...] = jnp.zeros(terms.shape, f32)
     wide_terms[...] = jnp.zeros(wide_terms.shape, f32)
     bias_terms[...] = jnp.zeros(bias_terms.shape, f32)
-    group = subparts * slots
-
-    def pick_cut(offset, unused):
-        at = pl.multiple_of(offset * group, 128)
-        table = edge_by_cell(cut_cells[:, pl.ds(at, group)], cell_count)
-        rows = dot(table, both[...]).astype(jnp.bfloat16)
-        own[pl.ds(offset * subparts, subparts)] = rows.reshape(subparts, slots, 2 * channels)
-        return unused
-
-    lax.fori_loop(0, 3, pick_cut, 0)
+    group = lists * slots
+
+    cut_table = edge_by_cell(cut_cells[...], cell_count)
+    own[...] = dot(cut_table, both[...]).astype(jnp.bfloat16).reshape(lists, slots, 2 * channels)
     incoming[subparts + subpart] = jnp.zeros((slots, 2 * channels), jnp.bfloat16)
     pl.semaphore_wait(barrier, total - 1)
 
@@ -243,9 +237,8 @@
 
     lax.fori_loop(0, lists, arrange, 0)
 
-    def cut(offset, unused):
-        at = pl.multiple_of(offset * group, 128)
-        rows = pl.ds(at, group)
+    def cut():
+        rows = pl.ds(0, group)
         live, lead = live_rows[rows], lead_rows[rows]
         inputs, hidden, flux, d_flux, d_before, d_inputs = edge_network(
             heads[rows], tails[rows], live,
@@ -263,9 +256,8 @@
             (d_before.astype(f32) * owned).astype(jnp.bfloat16),
             (d_flux.astype(f32) * owned).astype(jnp.bfloat16),
         )
-        return unused
-
-    lax.fori_loop(0, 3, cut, 0)
+
+    cut()
 
     terms[0:wide] = jnp.transpose(wide_terms[...])
     bias_rows = jnp.concatenate(

time: 30.7 us -> 31.2 us (1.016)
  Pallas kernels: 29.9 us -> 30.4 us
    pallas_call x1, Pallas kernels: 28 us -> 28.5 us  [local(): pl.pallas_call(functools.partial(layer_kernel, regions, subparts, chunk,...]
where the time goes in v5:
time: 31.2 us; the launch traced here: 31 us
  Pallas kernels  30.4 us (97%)
  between operations  0.64 us (2%)
    pallas_call x1, Pallas kernels, local(): pl.pallas_call(functools.partial(layer_kernel, regions, subparts, chunk,...  28.5 us
    pallas_call x1, Pallas kernels, local(): pl.pallas_call(hand_on, out_shape=[jax.ShapeDtypeStruct(result.shape, res...  1.91 us

profile of v5, /device:TPU:0, one launch (start us, length us, event | category | flops | bytes accessed | tf_op | source)
XLA Modules:
  0.0 31.0 jit_solution(7141244219611333691)
XLA Ops:
  0.6 28.5 %shard_map.136 = (bf16[1024,128]{1,0:T(8,128)(2,1)}, bf16[1024,128]{1,0:T(8,128)(2,1)}, f32[256,128]{1,0:T(8,128)}, f32[1,128]{1,0:T(1,128)}, f32[128,128]{1,0:T(8,128)}, /*index=5*/f32[1,128]{1,0:T(1,128)}) custom-call(bf16[1024,128]{1,0:T(8,128)(2,1)} %latents_from.1, bf16[1024,128]{1,0:T(8,128)(2,1)} %cotangent_from.1, s32[2,3072]{1,0:T(2,128)} %edges_from.1, ...), custom_call_target="tpu_custom_call" | custom-call | tf_op jit(solution)/shard_map/pallas_call | solution.py:359
  29.1 1.9 %shard_map.137 = (bf16[1024,128]{1,0:T(8,128)(2,1)}, bf16[1024,128]{1,0:T(8,128)(2,1)}, f32[256,128]{1,0:T(8,128)}, f32[1,128]{1,0:T(1,128)}, f32[128,128]{1,0:T(8,128)}, /*index=5*/f32[1,128]{1,0:T(1,128)}) custom-call(bf16[1024,128]{1,0:T(8,128)(2,1)} %get-tuple-element.18.refs_0_, bf16[1024,128]{1,0:T(8,128)(2,1)} %get-tuple-element.19.refs_1_, ...), custom_call_target="tpu_custom_call" | custom-call | tf_op jit(solution)/shard_map/pallas_call | solution.py:409
